TPU v7x, 32 devices: a whole 2x2x4 slice. The times are simulated.
32 devices in a mesh: section: 2 (over core), seq: 4 (over z), tp: 4 (over y, x).
Axes of the slice: x: 2, y: 2, z: 4, core: 2. Of those that a mesh axis runs over, the one named last changes fastest.
Arguments:
- hidden: bfloat16 [2, 2, 1, 1024, 768], P('section', None, None, 'seq'), may hold values from -6 to 6
- segments: int32 [2, 2, 1, 1024], replicated, may hold values from 0 to 2, as said below
- self_qkv: bfloat16 [2, 3, 768, 768], P('section', None, None, 'tp'), may hold values from -0.21875 to 0.21875
- self_out: bfloat16 [2, 768, 768], P('section', 'tp'), may hold values from -0.4375 to 0.4375
- ffn_in: bfloat16 [2, 768, 3072], P('section', None, 'tp'), may hold values from -0.21875 to 0.21875
- ffn_in_bias: float32 [2, 4, 768], P('section', 'tp'), may hold values from -3 to 3
- ffn_out: bfloat16 [2, 3072, 768], P('section', 'tp'), may hold values from -0.109375 to 0.109375
- norm_gains: float32 [2, 2, 768], P('section'), may hold values from 0.25 to 1.75
- norm_shifts: float32 [2, 3, 768], P('section'), may hold values from -2 to 2
- cross_qkv: bfloat16 [3, 768, 768], P(None, None, 'tp'), may hold values from -0.21875 to 0.21875
- cross_out: bfloat16 [768, 768], P('tp'), may hold values from -0.4375 to 0.4375
- cross_gain: float32 [768], replicated, may hold values from 0.25 to 1.75
- cross_shift: float32 [768], replicated, may hold values from -2 to 2
- cotangent: bfloat16 [2, 1, 1024, 768], P(None, None, 'seq'), may hold values from -6 to 6
Outputs:
- layer_out: bfloat16 [2, 2, 1, 1024, 768], P('section', None, None, 'seq')
- grad_hidden: bfloat16 [2, 2, 1, 1024, 768], P('section', None, None, 'seq')
- grad_self_qkv: float32 [2, 3, 768, 768], P('section', None, 'seq', 'tp')
- grad_self_out: float32 [2, 768, 768], P('section', 'tp', 'seq')
- grad_ffn_in: float32 [2, 768, 3072], P('section', 'seq', 'tp')
- grad_ffn_in_bias: float32 [2, 4, 768], P('section', 'tp', 'seq')
- grad_ffn_out: float32 [2, 3072, 768], P('section', 'tp', 'seq')
- grad_norm_gains: float32 [2, 2, 768], P('section', None, 'seq')
- grad_norm_shifts: float32 [2, 3, 768], P('section', None, 'seq')
- grad_cross_qkv: float32 [3, 768, 768], P(None, ('section', 'seq'), 'tp')
- grad_cross_out: float32 [768, 768], P('tp', ('section', 'seq'))
- grad_cross_gain: float32 [768], P(('section', 'seq'))
- grad_cross_shift: float32 [768], P(('section', 'seq'))
Inputs may be any that keep to these rules, and one draw needn't show every extreme that they name: `segments`: along each row of either side the ids never fall, and every row of both sides holds all three ids.
All inputs are finite; a program needn't handle non-finite values.
Results may differ from a plain program's by a relative error of at most 0.015.
Values may be sent and summed in bfloat16 or wider, within the bound.
No kernel may reach another device: no remote copies, remote signals or barrier semaphores. Data moves between devices by JAX's collectives and lax.ppermute only.
A program may use at most 192 MiB of HBM per device.

v0:
```python
import math

import jax
import jax.numpy as jnp
from jax import lax
from jax.sharding import PartitionSpec as P

HEAD_DIM = 64


epsilon = 1e-05
masked_out = -1e30


def for_sending(array):
    return jax.tree.map(lambda a: a.astype(jnp.bfloat16) if a.dtype == jnp.float32 else a, array)


def from_behind(block, axis, distance):
    devices = range(lax.axis_size(axis))
    route = [(i - distance, i) for i in devices if i - distance in devices]
    return lax.ppermute(block, axis, route)


def norm_apply(values, norm_gain, norm_shift):
    centred = values - jnp.mean(values, axis=-1, keepdims=True)
    spread = jnp.mean(centred * centred, axis=-1, keepdims=True)
    return centred * lax.rsqrt(spread + epsilon) * norm_gain + norm_shift


def norm_back(values, norm_gain, norm_shift, upstream):
    result, pullback = jax.vjp(norm_apply, values, norm_gain, norm_shift)
    return pullback(upstream)


def gelu_exact(values):
    return jax.nn.gelu(values, approximate=False)


def linear(values, weight):
    return jnp.einsum("rtd,de->rte", values, weight, preferred_element_type=jnp.float32)


def linear_back(grads_in, weight):
    return jnp.einsum("rte,de->rtd", grads_in, weight, preferred_element_type=jnp.float32)


def weight_grad(values, grads_in):
    return jnp.einsum("rtd,rte->de", values, grads_in, preferred_element_type=jnp.float32)


def build_mask(query_ids, key_ids, query_start, key_start, causal):
    query_places = query_start + jnp.arange(query_ids.shape[1])
    key_places = key_start + jnp.arange(key_ids.shape[1])
    same_doc = query_ids[:, :, None] == key_ids[:, None, :]
    earlier = key_places[None, None, :] <= query_places[None, :, None]
    return same_doc & (earlier | jnp.logical_not(causal))


def split_heads(values):
    return values.reshape(values.shape[0], values.shape[1], values.shape[2] // HEAD_DIM, HEAD_DIM)


def head_scores(query_heads, key_heads, allowed):
    scores = jnp.einsum(
        "rqhd,rkhd->rhqk", query_heads, key_heads, preferred_element_type=jnp.float32
    ) * (1.0 / math.sqrt(HEAD_DIM))
    return jnp.where(allowed[:, None], scores, masked_out)


def attend_forward(queries, keys_values, allowed):
    head_width = queries.shape[2]
    query_heads = split_heads(queries)
    key_heads = split_heads(keys_values[:, :, :head_width])
    value_heads = split_heads(keys_values[:, :, head_width:])
    scores = head_scores(query_heads, key_heads, allowed)
    largest = jnp.max(scores, axis=-1, keepdims=True)
    exp_total = jnp.sum(jnp.exp(scores - largest), axis=-1, keepdims=True)
    log_total = largest + jnp.log(exp_total)
    weights = jnp.exp(scores - log_total).astype(jnp.bfloat16)
    mixture = jnp.einsum(
        "rhqk,rkhd->rqhd", weights, value_heads, preferred_element_type=jnp.float32
    )
    return (mixture.reshape(queries.shape[0], queries.shape[1], head_width), log_total)


def attend_backward(queries, keys_values, allowed, log_total, grad_mixture):
    score_scale = 1.0 / math.sqrt(HEAD_DIM)
    head_width = queries.shape[2]
    query_heads = split_heads(queries)
    key_heads = split_heads(keys_values[:, :, :head_width])
    value_heads = split_heads(keys_values[:, :, head_width:])
    grad_heads = split_heads(grad_mixture)
    soft_weights = jnp.exp(head_scores(query_heads, key_heads, allowed) - log_total)
    grad_probs = jnp.einsum(
        "rqhd,rkhd->rhqk", grad_heads, value_heads, preferred_element_type=jnp.float32
    )
    row_inner = jnp.sum(soft_weights * grad_probs, axis=-1, keepdims=True)
    grad_scores = (soft_weights * (grad_probs - row_inner)).astype(jnp.bfloat16)
    grad_queries = (
        jnp.einsum("rhqk,rkhd->rqhd", grad_scores, key_heads, preferred_element_type=jnp.float32)
        * score_scale
    )
    grad_queries = grad_queries.reshape(queries.shape)
    return (grad_queries, None, row_inner)


def key_gradients(
    queries,
    gathered,
    local_kv,
    allowed,
    log_total,
    grad_mixture,
    query_ids,
    own_ids,
    own_start,
    causal,
):
    score_scale = 1.0 / math.sqrt(HEAD_DIM)
    grad_queries, unused, row_inner = attend_backward(
        queries, gathered, allowed, log_total, grad_mixture
    )
    all_log, all_inner = (
        lax.all_gather(log_total, "seq", axis=2, tiled=True),
        lax.all_gather(row_inner, "seq", axis=2, tiled=True),
    )
    head_width = queries.shape[2]
    own_keys = split_heads(local_kv[:, :, :head_width])
    own_values = split_heads(local_kv[:, :, head_width:])
    empty = jnp.zeros(own_keys.shape, jnp.float32)
    start = jnp.int32(0)
    query_piece = lax.all_gather(for_sending(queries), "seq", axis=1, tiled=True)
    grad_piece = lax.all_gather(grad_mixture, "seq", axis=1, tiled=True)
    count = query_piece.shape[1]
    log_piece = lax.dynamic_slice_in_dim(all_log, start, count, 2)
    inner_piece = lax.dynamic_slice_in_dim(all_inner, start, count, 2)
    piece_ids = lax.dynamic_slice_in_dim(query_ids, start, count, 1)
    piece_allowed = build_mask(piece_ids, own_ids, start, own_start, causal)
    piece_heads = split_heads(query_piece)
    grad_heads = split_heads(grad_piece)
    soft_weights = jnp.exp(head_scores(piece_heads, own_keys, piece_allowed) - log_piece)
    grad_probs = jnp.einsum(
        "rqhd,rkhd->rhqk", grad_heads, own_values, preferred_element_type=jnp.float32
    )
    grad_scores = (soft_weights * (grad_probs - inner_piece)).astype(jnp.bfloat16)
    new_keys = (
        empty
        + jnp.einsum(
            "rhqk,rqhd->rkhd", grad_scores, piece_heads, preferred_element_type=jnp.float32
        )
        * score_scale
    )
    new_values = empty + jnp.einsum(
        "rhqk,rqhd->rkhd",
        soft_weights.astype(jnp.bfloat16),
        grad_heads,
        preferred_element_type=jnp.float32,
    )
    row_shape = (queries.shape[0], queries.shape[1], head_width)
    return (
        grad_queries,
        jnp.concatenate([new_keys.reshape(row_shape), new_values.reshape(row_shape)], axis=-1),
    )


def add_members(total, fresh):
    if total is None:
        return fresh
    return tuple((left + right for left, right in zip(total, fresh)))


def on_device(
    hidden,
    segments,
    self_qkv,
    self_out,
    ffn_in,
    ffn_in_bias,
    ffn_out,
    norm_gains,
    norm_shifts,
    cross_qkv,
    cross_out,
    cross_gain,
    cross_shift,
    cotangent,
):
    section_index = lax.axis_index("section")
    seq_index = lax.axis_index("seq")
    decoding = section_index == 1
    micro_count = hidden.shape[1]
    span_len = hidden.shape[3]
    own_start = seq_index * span_len
    side_ids = lax.dynamic_index_in_dim(segments, section_index, 0, keepdims=False)
    qkv_weight = self_qkv[0]
    head_width = qkv_weight.shape[2]
    self_kv_weight = jnp.concatenate([qkv_weight[1], qkv_weight[2]], axis=1)
    out_weight = self_out[0]
    weight_in = ffn_in[0]
    bias_in = ffn_in_bias[0, 0]
    weight_out = ffn_out[0]
    gain_rows = norm_gains[0]
    shift_rows = norm_shifts[0]
    cross_kv_weight = jnp.concatenate([cross_qkv[1], cross_qkv[2]], axis=1)

    def share_keys(local_kv):
        return lax.all_gather(local_kv, "seq", axis=1, tiled=True)

    def head_total(partial_value):
        return lax.psum(partial_value, "tp")

    memory = jnp.zeros(hidden.shape[2:], jnp.bfloat16)
    outputs = jnp.zeros(hidden.shape[1:], jnp.bfloat16)
    saved_steps = []
    for moment in range(micro_count + 1):
        offset = moment - section_index
        active = (offset >= 0) & (offset < micro_count)
        micro_index = jnp.clip(offset, 0, micro_count - 1)
        inputs_bf = lax.dynamic_index_in_dim(hidden[0], micro_index, 0, keepdims=False)
        inputs = inputs_bf.astype(jnp.float32)
        row_ids = lax.dynamic_index_in_dim(side_ids, micro_index, 0, keepdims=False)
        memory_ids = lax.dynamic_index_in_dim(segments[0], micro_index, 0, keepdims=False)
        own_ids = lax.dynamic_slice_in_dim(row_ids, own_start, span_len, 1)
        own_memory_ids = lax.dynamic_slice_in_dim(memory_ids, own_start, span_len, 1)
        queries = linear(inputs_bf, qkv_weight[0]).astype(jnp.bfloat16)
        local_kv = linear(inputs_bf, self_kv_weight).astype(jnp.bfloat16)
        gathered = share_keys(local_kv)
        allowed = build_mask(own_ids, row_ids, own_start, 0, decoding)
        mixture, log_total = attend_forward(queries, gathered, allowed)
        mixture_bf = mixture.astype(jnp.bfloat16)
        attn_sum = inputs + head_total(linear(mixture_bf, out_weight))
        after_self = norm_apply(attn_sum, gain_rows[0], shift_rows[0])
        after_self_bf = after_self.astype(jnp.bfloat16)
        cross_queries = linear(after_self_bf, cross_qkv[0]).astype(jnp.bfloat16)
        cross_local = linear(memory, cross_kv_weight).astype(jnp.bfloat16)
        cross_gathered = share_keys(cross_local)
        cross_allowed = build_mask(own_ids, memory_ids, own_start, 0, False)
        cross_mixture, cross_log = attend_forward(cross_queries, cross_gathered, cross_allowed)
        cross_bf = cross_mixture.astype(jnp.bfloat16)
        cross_sum = after_self + head_total(linear(cross_bf, cross_out))
        after_cross = jnp.where(
            decoding, norm_apply(cross_sum, cross_gain, cross_shift), after_self
        )
        after_cross_bf = after_cross.astype(jnp.bfloat16)
        before_act = linear(after_cross_bf, weight_in) + bias_in
        activated_bf = gelu_exact(before_act).astype(jnp.bfloat16)
        ffn_sum = after_cross + head_total(linear(activated_bf, weight_out)) + shift_rows[2]
        result = norm_apply(ffn_sum, gain_rows[1], shift_rows[1])
        result_bf = result.astype(jnp.bfloat16)
        current = lax.dynamic_index_in_dim(outputs, micro_index, 0, keepdims=False)
        outputs = lax.dynamic_update_index_in_dim(
            outputs, jnp.where(active, result_bf, current), micro_index, 0
        )
        saved_steps.append(
            dict(
                inputs_bf=inputs_bf,
                row_ids=row_ids,
                own_ids=own_ids,
                own_memory_ids=own_memory_ids,
                memory=memory,
                queries=queries,
                local_kv=local_kv,
                gathered=gathered,
                allowed=allowed,
                log_total=log_total,
                mixture_bf=mixture_bf,
                attn_sum=attn_sum,
                after_self_bf=after_self_bf,
                cross_queries=cross_queries,
                cross_local=cross_local,
                cross_gathered=cross_gathered,
                cross_allowed=cross_allowed,
                cross_log=cross_log,
                cross_bf=cross_bf,
                cross_sum=cross_sum,
                after_cross_bf=after_cross_bf,
                before_act=before_act,
                activated_bf=activated_bf,
                ffn_sum=ffn_sum,
            )
        )
        if moment < micro_count:
            memory = from_behind(result_bf, "section", 1)
    grad_inputs = jnp.zeros(hidden.shape[1:], jnp.bfloat16)
    received = jnp.zeros(hidden.shape[2:], jnp.bfloat16)
    section_total = None
    cross_total = None
    for moment in range(micro_count + 1):
        saved = saved_steps[micro_count - moment]
        offset = micro_count - moment - section_index
        active = (offset >= 0) & (offset < micro_count)
        scale_active = active.astype(jnp.float32)
        micro_index = jnp.clip(offset, 0, micro_count - 1)
        upstream_dec = lax.dynamic_index_in_dim(cotangent, micro_index, 0, keepdims=False).astype(
            jnp.float32
        )
        upstream = jnp.where(decoding, upstream_dec, received.astype(jnp.float32))
        grad_ffn_sum, grad_gain_two, grad_shift_two = norm_back(
            saved["ffn_sum"], gain_rows[1], shift_rows[1], upstream
        )
        grad_bias_out = jnp.sum(grad_ffn_sum, axis=(0, 1))
        grad_branch_bf = grad_ffn_sum.astype(jnp.bfloat16)
        grad_weight_out = weight_grad(saved["activated_bf"], grad_branch_bf)
        grad_act = linear_back(grad_branch_bf, weight_out)
        unused, gelu_pull = jax.vjp(gelu_exact, saved["before_act"])
        grad_before = gelu_pull(grad_act)[0].astype(jnp.bfloat16)
        grad_bias_in = jnp.sum(grad_before.astype(jnp.float32), axis=(0, 1))
        grad_weight_in = weight_grad(saved["after_cross_bf"], grad_before)
        grad_after_cross = grad_ffn_sum + lax.psum(linear_back(grad_before, weight_in), "tp")
        grad_cross_sum, grad_cross_gain, grad_cross_shift = norm_back(
            saved["cross_sum"], cross_gain, cross_shift, grad_after_cross
        )
        grad_cross_sum = jnp.where(decoding, grad_cross_sum, 0.0)
        grad_cross_gain = jnp.where(decoding, grad_cross_gain, 0.0)
        grad_cross_shift = jnp.where(decoding, grad_cross_shift, 0.0)
        grad_cross_bf = grad_cross_sum.astype(jnp.bfloat16)
        grad_cross_out = weight_grad(saved["cross_bf"], grad_cross_bf)
        grad_cross_mix = linear_back(grad_cross_bf, cross_out).astype(jnp.bfloat16)
        grad_cross_queries, grad_cross_kv = key_gradients(
            saved["cross_queries"],
            saved["cross_gathered"],
            saved["cross_local"],
            saved["cross_allowed"],
            saved["cross_log"],
            grad_cross_mix,
            saved["row_ids"],
            saved["own_memory_ids"],
            own_start,
            False,
        )
        grad_cross_queries_bf = grad_cross_queries.astype(jnp.bfloat16)
        grad_cross_kv_bf = grad_cross_kv.astype(jnp.bfloat16)
        grad_cross_q_weight = weight_grad(saved["after_self_bf"], grad_cross_queries_bf)
        grad_cross_kv_weight = weight_grad(saved["memory"], grad_cross_kv_bf)
        grad_self_part, grad_memory = lax.psum(
            (
                linear_back(grad_cross_queries_bf, cross_qkv[0]),
                linear_back(grad_cross_kv_bf, cross_kv_weight),
            ),
            "tp",
        )
        grad_after_self = jnp.where(decoding, grad_cross_sum, grad_after_cross) + grad_self_part
        grad_memory_bf = grad_memory.astype(jnp.bfloat16)
        grad_attn_sum, grad_gain_one, grad_shift_one = norm_back(
            saved["attn_sum"], gain_rows[0], shift_rows[0], grad_after_self
        )
        grad_attn_bf = grad_attn_sum.astype(jnp.bfloat16)
        grad_out_weight = weight_grad(saved["mixture_bf"], grad_attn_bf)
        grad_mix = linear_back(grad_attn_bf, out_weight).astype(jnp.bfloat16)
        grad_queries, grad_kv = key_gradients(
            saved["queries"],
            saved["gathered"],
            saved["local_kv"],
            saved["allowed"],
            saved["log_total"],
            grad_mix,
            saved["row_ids"],
            saved["own_ids"],
            own_start,
            decoding,
        )
        grad_queries_bf = grad_queries.astype(jnp.bfloat16)
        grad_kv_bf = grad_kv.astype(jnp.bfloat16)
        grad_q_weight = weight_grad(saved["inputs_bf"], grad_queries_bf)
        grad_kv_weight = weight_grad(saved["inputs_bf"], grad_kv_bf)
        grad_now = grad_attn_sum + lax.psum(
            linear_back(grad_queries_bf, qkv_weight[0]) + linear_back(grad_kv_bf, self_kv_weight),
            "tp",
        )
        current_grad = lax.dynamic_index_in_dim(grad_inputs, micro_index, 0, keepdims=False)
        grad_inputs = lax.dynamic_update_index_in_dim(
            grad_inputs,
            jnp.where(active, grad_now.astype(jnp.bfloat16), current_grad),
            micro_index,
            0,
        )
        if moment < micro_count:
            received = from_behind(grad_memory_bf, "section", -1)
        section_now = (
            jnp.stack(
                [grad_q_weight, grad_kv_weight[:, :head_width], grad_kv_weight[:, head_width:]]
            )[None]
            * scale_active,
            grad_out_weight[None] * scale_active,
            grad_weight_in[None] * scale_active,
            grad_bias_in[None, None] * scale_active,
            grad_weight_out[None] * scale_active,
            jnp.stack([grad_gain_one, grad_gain_two])[None] * scale_active,
            jnp.stack([grad_shift_one, grad_shift_two, grad_bias_out])[None] * scale_active,
        )
        cross_now = (
            jnp.stack(
                [
                    grad_cross_q_weight,
                    grad_cross_kv_weight[:, :head_width],
                    grad_cross_kv_weight[:, head_width:],
                ]
            )
            * scale_active,
            grad_cross_out * scale_active,
            grad_cross_gain * scale_active,
            grad_cross_shift * scale_active,
        )
        section_total = add_members(section_total, section_now)
        cross_total = add_members(cross_total, cross_now)
    return (
        outputs[None],
        grad_inputs[None],
        lax.psum_scatter(section_total[0], "seq", scatter_dimension=2, tiled=True),
        lax.psum_scatter(section_total[1], "seq", scatter_dimension=2, tiled=True),
        lax.psum_scatter(section_total[2], "seq", scatter_dimension=1, tiled=True),
        lax.psum_scatter(section_total[3], "seq", scatter_dimension=2, tiled=True),
        lax.psum_scatter(section_total[4], "seq", scatter_dimension=2, tiled=True),
        lax.psum_scatter(section_total[5], "seq", scatter_dimension=2, tiled=True),
        lax.psum_scatter(section_total[6], "seq", scatter_dimension=2, tiled=True),
        lax.psum_scatter(cross_total[0], ("section", "seq"), scatter_dimension=1, tiled=True),
        lax.psum_scatter(cross_total[1], ("section", "seq"), scatter_dimension=1, tiled=True),
        lax.psum_scatter(cross_total[2], ("section", "seq"), scatter_dimension=0, tiled=True),
        lax.psum_scatter(cross_total[3], ("section", "seq"), scatter_dimension=0, tiled=True),
    )


def solution(mesh):
    return jax.shard_map(
        on_device,
        mesh=mesh,
        in_specs=(
            P("section", None, None, "seq", None),
            P(),
            P("section", None, None, "tp"),
            P("section", "tp", None),
            P("section", None, "tp"),
            P("section", "tp", None),
            P("section", "tp", None),
            P("section", None, None),
            P("section", None, None),
            P(None, None, "tp"),
            P("tp", None),
            P(),
            P(),
            P(None, None, "seq", None),
        ),
        out_specs=(
            P("section", None, None, "seq", None),
            P("section", None, None, "seq", None),
            P("section", None, "seq", "tp"),
            P("section", "tp", "seq"),
            P("section", "seq", "tp"),
            P("section", "tp", "seq"),
            P("section", "tp", "seq"),
            P("section", None, "seq"),
            P("section", None, "seq"),
            P(None, ("section", "seq"), "tp"),
            P("tp", ("section", "seq")),
            P(("section", "seq")),
            P(("section", "seq")),
        ),
        check_vma=False,
    )
```

profile of v0, /device:TPU:0, one launch (start us, length us, event | category | flops | bytes accessed | tf_op | source)
XLA Modules:
  0.0 1419.1 jit_solution(10439486005516296048)
XLA Ops:
  13.9 21.3 %all-gather = bf16[1024,384]{1,0:T(8,128)(2,1)S(1)} all-gather(bf16[256,384]{1,0:T(8,128)(2,1)S(1)} %convolution_convert_fusion.5), channel_id=2, replica_groups=mesh['section'=2,'seq'=4,'tp'=4] {'seq'}, dimensions={0}, use_global_device_ids=true | all-gather | bytes 983040 | tf_op jit(solution)/shard_map/all_gather | solution.py:208
  45.7 17.7 %all-gather.1 = bf16[1024,384]{1,0:T(8,128)(2,1)S(1)} all-gather(bf16[256,384]{1,0:T(8,128)(2,1)S(1)} %convolution_convert_fusion.4), channel_id=3, replica_groups=mesh['section'=2,'seq'=4,'tp'=4] {'seq'}, dimensions={0}, use_global_device_ids=true | all-gather | bytes 983040 | tf_op jit(solution)/shard_map/all_gather | solution.py:208
  64.5 17.5 %all-gather.2 = bf16[1024,384]{1,0:T(8,128)(2,1)S(1)} all-gather(bf16[256,384]{1,0:T(8,128)(2,1)S(1)} %convolution_convert_fusion.3), channel_id=4, replica_groups=mesh['section'=2,'seq'=4,'tp'=4] {'seq'}, dimensions={0}, use_global_device_ids=true | all-gather | bytes 983040 | tf_op jit(solution)/shard_map/all_gather | solution.py:208
  108.8 39.2 %all-reduce.26.cloned.1.call-done = f32[1,256,768]{2,1,0:T(8,128)} async-done(((f32[1,256,768]{2,1,0:T(8,128)}), f32[1,256,768]{2,1,0:T(8,128)}) %all-reduce.26.cloned.1.call-update) | async-done | bytes 786448 | tf_op jit(solution)/shard_map/psum | solution.py:211
  150.1 3.1 multiply_convert_fusion.44
  156.6 19.6 %all-gather.4 = bf16[1024,384]{1,0:T(8,128)(2,1)S(1)} all-gather(bf16[256,384]{1,0:T(8,128)(2,1)S(1)} %convolution_convert_fusion.1), channel_id=6, replica_groups=mesh['section'=2,'seq'=4,'tp'=4] {'seq'}, dimensions={0}, use_global_device_ids=true | all-gather | bytes 983040 | tf_op jit(solution)/shard_map/all_gather | solution.py:208
  180.8 3.5 fusion.4
  184.3 32.3 %all-reduce.48.cloned.1.call-done = (f32[1,256,768]{2,1,0:T(8,128)}, f32[1,256,768]{2,1,0:T(8,128)}) async-done(((f32[1,256,768]{2,1,0:T(8,128)}, f32[1,256,768]{2,1,0:T(8,128)}), (f32[1,256,768]{2,1,0:T(8,128)}, f32[1,256,768]{2,1,0:T(8,128)})) %all-reduce.48.cloned.1.call-update) | async-done | bytes 1572880 | tf_op jit(solution)/shard_map/psum | solution.py:211
  223.6 20.1 %all-gather.3 = bf16[1024,384]{1,0:T(8,128)(2,1)S(1)} all-gather(bf16[256,384]{1,0:T(8,128)(2,1)S(1)} %convolution_convert_fusion.2), channel_id=5, replica_groups=mesh['section'=2,'seq'=4,'tp'=4] {'seq'}, dimensions={0}, use_global_device_ids=true | all-gather | bytes 983040 | tf_op jit(solution)/shard_map/all_gather | solution.py:208
  261.9 39.4 %all-reduce.28.cloned.1.call-done = f32[1,256,768]{2,1,0:T(8,128)} async-done(((f32[1,256,768]{2,1,0:T(8,128)}), f32[1,256,768]{2,1,0:T(8,128)}) %all-reduce.28.cloned.1.call-update) | async-done | bytes 786448 | tf_op jit(solution)/shard_map/psum | solution.py:211
  309.7 60.4 %all-reduce.46.cloned.1.call-done = (f32[1,256,768]{2,1,0:T(8,128)}, f32[1,256,768]{2,1,0:T(8,128)}) async-done(((f32[1,256,768]{2,1,0:T(8,128)}, f32[1,256,768]{2,1,0:T(8,128)}), (f32[1,256,768]{2,1,0:T(8,128)}, f32[1,256,768]{2,1,0:T(8,128)})) %all-reduce.46.cloned.1.call-update) | async-done | bytes 1572880 | tf_op jit(solution)/shard_map/psum | solution.py:211
  379.0 19.8 %all-gather.5 = bf16[1024,384]{1,0:T(8,128)(2,1)S(1)} all-gather(bf16[256,384]{1,0:T(8,128)(2,1)S(1)} %convolution_convert_fusion), channel_id=7, replica_groups=mesh['section'=2,'seq'=4,'tp'=4] {'seq'}, dimensions={0}, use_global_device_ids=true | all-gather | bytes 983040 | tf_op jit(solution)/shard_map/all_gather | solution.py:208
  414.0 15.8 %all-gather.6 = bf16[1024,192]{0,1:T(8,128)(2,1)} all-gather(bf16[256,192]{0,1:T(8,128)(2,1)} %copy-done.215), channel_id=8, replica_groups=mesh['section'=2,'seq'=4,'tp'=4] {'seq'}, dimensions={0}, use_global_device_ids=true | all-gather | bytes 491520 | tf_op jit(solution)/shard_map/all_gather | solution.py:133
  429.8 28.0 %all-reduce.30.cloned.1.call-done = f32[1,256,768]{2,1,0:T(8,128)} async-done(((f32[1,256,768]{2,1,0:T(8,128)}), f32[1,256,768]{2,1,0:T(8,128)}) %all-reduce.30.cloned.1.call-update) | async-done | bytes 786448 | tf_op jit(solution)/shard_map/psum | solution.py:211
  466.1 3.1 fusion.462
  471.7 42.3 %all-reduce.32.cloned.1.call-done = f32[1,256,768]{2,1,0:T(8,128)} async-done(((f32[1,256,768]{2,1,0:T(8,128)}), f32[1,256,768]{2,1,0:T(8,128)}) %all-reduce.32.cloned.1.call-update) | async-done | bytes 786448 | tf_op jit(solution)/shard_map/psum | solution.py:211
  523.5 16.5 %all-gather.10 = bf16[1024,192]{0,1:T(8,128)(2,1)} all-gather(bf16[256,192]{0,1:T(8,128)(2,1)} %convolution_convert_fusion.12), channel_id=12, replica_groups=mesh['section'=2,'seq'=4,'tp'=4] {'seq'}, dimensions={0}, use_global_device_ids=true | all-gather | bytes 491520 | tf_op jit(solution)/shard_map/all_gather | solution.py:133
  545.1 14.1 all-gather.11
  559.2 3.3 fusion.463
  562.5 6.4 all-reduce.34.cloned.1.call-done
  574.5 14.5 %all-gather.12 = bf16[1024,192]{0,1:T(8,128)(2,1)S(1)} all-gather(bf16[256,192]{0,1:T(8,128)(2,1)S(1)} %convolution_convert_fusion.11), channel_id=14, replica_groups=mesh['section'=2,'seq'=4,'tp'=4] {'seq'}, dimensions={0}, use_global_device_ids=true | all-gather | bytes 491520 | tf_op jit(solution)/shard_map/all_gather | solution.py:134
  591.9 14.1 all-gather.13
  607.6 4.0 fusion.154
  614.2 29.7 %all-reduce.49 = bf16[1,256,768]{2,1,0:T(8,128)(2,1)} all-reduce(f32[1,256,768]{2,1,0:T(8,128)} %convolution_bitcast_fusion.7), channel_id=1, replica_groups=mesh['section'=2,'seq'=4,'tp'=4] {'tp'}, use_global_device_ids=true, to_apply=%region_50.51 | all-reduce | flops 196608 | bytes 1179648 | tf_op jit(solution)/shard_map/psum | solution.py:336
  645.3 16.8 %all-gather.14 = bf16[1024,192]{0,1:T(8,128)(2,1)S(1)} all-gather(bf16[256,192]{0,1:T(8,128)(2,1)} %copy-done.212), channel_id=16, replica_groups=mesh['section'=2,'seq'=4,'tp'=4] {'seq'}, dimensions={0}, use_global_device_ids=true | all-gather | bytes 491520 | tf_op jit(solution)/shard_map/all_gather | solution.py:133
  662.2 3.3 fusion.464
  671.3 14.7 %all-gather.18 = bf16[1024,192]{0,1:T(8,128)(2,1)S(1)} all-gather(bf16[256,192]{0,1:T(8,128)(2,1)S(1)} %copy-done.214), channel_id=20, replica_groups=mesh['section'=2,'seq'=4,'tp'=4] {'seq'}, dimensions={0}, use_global_device_ids=true | all-gather | bytes 491520 | tf_op jit(solution)/shard_map/all_gather | solution.py:133
  688.5 13.7 all-gather.19
  704.6 14.0 all-reduce.36.cloned.1.call-done
  722.2 14.5 %all-gather.20 = bf16[1024,192]{0,1:T(8,128)(2,1)S(1)} all-gather(bf16[256,192]{0,1:T(8,128)(2,1)S(1)} %convolution_convert_fusion.9), channel_id=22, replica_groups=mesh['section'=2,'seq'=4,'tp'=4] {'seq'}, dimensions={0}, use_global_device_ids=true | all-gather | bytes 491520 | tf_op jit(solution)/shard_map/all_gather | solution.py:134
  739.7 14.0 all-gather.21
  755.3 4.0 fusion.156
  761.8 29.8 %all-reduce.50 = bf16[1,256,768]{2,1,0:T(8,128)(2,1)} all-reduce(f32[1,256,768]{2,1,0:T(8,128)} %convolution_bitcast_fusion.6), channel_id=1, replica_groups=mesh['section'=2,'seq'=4,'tp'=4] {'tp'}, use_global_device_ids=true, to_apply=%region_62.63 | all-reduce | flops 196608 | bytes 1179648 | tf_op jit(solution)/shard_map/psum | solution.py:336
  793.1 16.6 %all-gather.22 = bf16[1024,192]{0,1:T(8,128)(2,1)S(1)} all-gather(bf16[256,192]{0,1:T(8,128)(2,1)S(1)} %copy-done.211), channel_id=24, replica_groups=mesh['section'=2,'seq'=4,'tp'=4] {'seq'}, dimensions={0}, use_global_device_ids=true | all-gather | bytes 491520 | tf_op jit(solution)/shard_map/all_gather | solution.py:133
  816.3 4.1 fusion.111
  824.8 40.2 %all-reduce.38.cloned.1.call-done = f32[1,256,768]{2,1,0:T(8,128)} async-done(((f32[1,256,768]{2,1,0:T(8,128)}), f32[1,256,768]{2,1,0:T(8,128)}) %all-reduce.38.cloned.1.call-update) | async-done | bytes 786448 | tf_op jit(solution)/shard_map/psum | solution.py:310
  880.2 13.6 all-gather.7
  893.8 13.7 all-gather.15
  907.5 13.5 all-gather.23
  921.1 13.7 all-gather.27
  934.8 14.2 %all-gather.26 = bf16[1024,192]{0,1:T(8,128)(2,1)S(1)} all-gather(bf16[256,192]{0,1:T(8,128)(2,1)S(1)} %copy-done.209), channel_id=28, replica_groups=mesh['section'=2,'seq'=4,'tp'=4] {'seq'}, dimensions={0}, use_global_device_ids=true | all-gather | bytes 491520 | tf_op jit(solution)/shard_map/all_gather | solution.py:133
  973.9 6.8 copy.126
  981.9 17.2 %all-gather.28 = bf16[1024,192]{0,1:T(8,128)(2,1)S(1)} all-gather(bf16[256,192]{0,1:T(8,128)(2,1)S(1)} %copy-done.166), channel_id=30, replica_groups=mesh['section'=2,'seq'=4,'tp'=4] {'seq'}, dimensions={0}, use_global_device_ids=true | all-gather | bytes 491520 | tf_op jit(solution)/shard_map/all_gather | solution.py:134
  999.1 13.8 all-gather.29
  1013.5 3.5 fusion.132
  1017.1 3.6 multiply_reduce_fusion.13
  1020.8 3.7 multiply_reduce_fusion.10
  1031.3 3.3 fusion.426
  1043.3 3.5 fusion.158
  1060.9 16.4 %all-gather.8 = bf16[1024,192]{0,1:T(8,128)(2,1)S(1)} all-gather(bf16[256,192]{0,1:T(8,128)(2,1)S(1)} %convolution_convert_fusion.10), channel_id=10, replica_groups=mesh['section'=2,'seq'=4,'tp'=4] {'seq'}, dimensions={0}, use_global_device_ids=true | all-gather | bytes 491520 | tf_op jit(solution)/shard_map/all_gather | solution.py:134
  1078.6 13.9 all-gather.9
  1096.0 17.5 %all-gather.16 = bf16[1024,192]{0,1:T(8,128)(2,1)} all-gather(bf16[256,192]{0,1:T(8,128)(2,1)S(1)} %convolution_convert_fusion.8), channel_id=18, replica_groups=mesh['section'=2,'seq'=4,'tp'=4] {'seq'}, dimensions={0}, use_global_device_ids=true | all-gather | bytes 491520 | tf_op jit(solution)/shard_map/all_gather | solution.py:134
  1116.5 13.8 all-gather.17
  1133.2 13.5 all-gather.25
  1148.3 4.2 fusion.153
  1152.6 17.0 %all-gather.24 = bf16[1024,192]{0,1:T(8,128)(2,1)} all-gather(bf16[256,192]{0,1:T(8,128)(2,1)} %copy-done.171), channel_id=26, replica_groups=mesh['section'=2,'seq'=4,'tp'=4] {'seq'}, dimensions={0}, use_global_device_ids=true | all-gather | bytes 491520 | tf_op jit(solution)/shard_map/all_gather | solution.py:134
  1172.3 4.4 fusion.114
  1180.5 4.3 fusion.155
  1187.5 3.3 fusion.116
  1193.3 3.4 fusion.157
  1217.1 17.4 %all-reduce.3 = (f32[768]{0:T(1024)S(1)}, f32[768]{0:T(1024)S(1)}) all-reduce(f32[768]{0:T(1024)S(1)} %get-tuple-element.260, f32[768]{0:T(1024)S(1)} %get-tuple-element.259), channel_id=41, replica_groups=mesh['section'=2,'seq'=4,'tp'=4] {'section','seq'}, use_global_device_ids=true, to_apply=%region_104.105.clone | all-reduce | flops 1536 | bytes 12288
  1246.9 71.1 %all-reduce.42.cloned.1.call-done = (f32[1,256,768]{2,1,0:T(8,128)}, f32[1,256,768]{2,1,0:T(8,128)}, f32[1,256,768]{2,1,0:T(8,128)}) async-done(((f32[1,256,768]{2,1,0:T(8,128)}, f32[1,256,768]{2,1,0:T(8,128)}, f32[1,256,768]{2,1,0:T(8,128)}), (f32[1,256,768]{2,1,0:T(8,128)}, f32[1,256,768]{2,1,0:T(8,128)}, f32[1,256,768]{2,1,0:T(8,128)})) %all-reduce.42.cloned.1.call-update) | async-done | bytes 2359312 | tf_op jit(solution)/shard_map/psum | solution.py:367
  1320.1 41.6 %reduce-scatter.25.cloned.1.call-done = f32[192,576]{1,0:T(8,128)} async-done(((f32[768,576]{1,0:T(8,128)}), f32[192,576]{1,0:T(8,128)}) %reduce-scatter.25.cloned.1.call-update) | async-done | bytes 442384
  1364.0 48.0 %reduce-scatter.23.cloned.1.call-done = f32[1,192,768]{2,1,0:T(8,128)} async-done(((f32[1,768,768]{2,1,0:T(8,128)}), f32[1,192,768]{2,1,0:T(8,128)}) %reduce-scatter.23.cloned.1.call-update) | async-done | bytes 589840 | tf_op jit(solution)/shard_map/reduce_scatter | solution.py:412
  (1136 shorter events, 312.8 us)
Async XLA Ops:
  7.2 142.9 %copy-start = (bf16[1,768,768]{2,1,0:T(8,128)(2,1)S(1)}, bf16[1,768,768]{2,1,0:T(8,128)(2,1)}, u32[]{:S(2)}) copy-start(bf16[1,768,768]{2,1,0:T(8,128)(2,1)} %param.18) | copy-start | bytes 3538948
  7.2 84.1 %all-reduce.24.cloned.1.call-start = ((), (), s32[]{:S(2)}) async-start(), calls=%async_computation.8 | async-start | bytes 1572864 | tf_op jit(solution)/shard_map/psum | solution.py:211
  38.6 50.2 %copy-start.84 = (pred[256,1024]{1,0:T(8,128)(4,1)}, pred[256,1024]{1,0:T(8,128)(4,1)S(1)}, u32[]{:S(2)}) copy-start(pred[256,1024]{1,0:T(8,128)(4,1)S(1)} %get-tuple-element.222) | copy-start | bytes 786436
  42.7 105.2 %all-reduce.26.cloned.1.call-start = ((), (), s32[]{:S(2)}) async-start(), calls=%async_computation.9 | async-start | bytes 1572864 | tf_op jit(solution)/shard_map/psum | solution.py:211
  87.5 129.2 %copy-start.243 = (f32[768]{0:T(1024)}, f32[768]{0:T(1024)S(1)}, u32[]{:S(2)}) copy-start(f32[768]{0:T(1024)S(1)} %get-tuple-element.80) | copy-start | bytes 9220
  87.5 130.9 %copy-start.240 = (f32[768]{0:T(1024)}, f32[768]{0:T(1024)S(1)}, u32[]{:S(2)}) copy-start(f32[768]{0:T(1024)S(1)} %get-tuple-element.78) | copy-start | bytes 9220
  92.6 57.1 %copy-start.13 = (f32[1,256,768]{2,1,0:T(8,128)}, f32[1,256,768]{2,1,0:T(8,128)S(1)}, u32[]{:S(2)}) copy-start(f32[1,256,768]{2,1,0:T(8,128)S(1)} %get-tuple-element.146) | copy-start | bytes 2359300
  92.6 57.1 %copy-start.260 = (f32[256]{0:T(256)}, f32[256]{0:T(256)S(1)}, u32[]{:S(2)}) copy-start(f32[256]{0:T(256)S(1)} %broadcast_multiply_fusion.8) | copy-start | bytes 3076
  92.9 56.8 %copy-start.269 = (f32[256]{0:T(256)}, f32[256]{0:T(256)S(1)}, u32[]{:S(2)}) copy-start(f32[256]{0:T(256)S(1)} %fusion.330) | copy-start | bytes 3076
  99.4 117.2 %all-reduce.48.cloned.1.call-start = ((), (), s32[]{:S(2)}) async-start(), calls=%async_computation.28 | async-start | bytes 3145728 | tf_op jit(solution)/shard_map/psum | solution.py:211
  104.5 198.9 %copy-start.375 = (f32[768]{0:T(1024)}, f32[768]{0:T(1024)S(1)}, u32[]{:S(2)}) copy-start(f32[768]{0:T(1024)S(1)} %reduce.99) | copy-start | bytes 9220
  155.5 145.9 %all-reduce.28.cloned.1.call-start = ((), (), s32[]{:S(2)}) async-start(), calls=%async_computation.10 | async-start | bytes 1572864 | tf_op jit(solution)/shard_map/psum | solution.py:211
  218.7 3.7 collective-permute-start
  220.7 82.4 %copy-start.15 = (f32[1,256,768]{2,1,0:T(8,128)}, f32[1,256,768]{2,1,0:T(8,128)S(1)}, u32[]{:S(2)}) copy-start(f32[1,256,768]{2,1,0:T(8,128)S(1)} %get-tuple-element.136) | copy-start | bytes 2359300
  220.7 82.4 %copy-start.263 = (f32[256]{0:T(256)}, f32[256]{0:T(256)S(1)}, u32[]{:S(2)}) copy-start(f32[256]{0:T(256)S(1)} %broadcast_multiply_fusion.5) | copy-start | bytes 3076
  220.9 82.1 %copy-start.272 = (f32[256]{0:T(256)}, f32[256]{0:T(256)S(1)}, u32[]{:S(2)}) copy-start(f32[256]{0:T(256)S(1)} %fusion.333) | copy-start | bytes 3076
  253.9 116.1 %all-reduce.46.cloned.1.call-start = ((), (), s32[]{:S(2)}) async-start(), calls=%async_computation.27 | async-start | bytes 3145728 | tf_op jit(solution)/shard_map/psum | solution.py:211
  307.5 62.6 %copy-start.63 = (f32[1,256,768]{2,1,0:T(8,128)S(1)}, f32[1,256,768]{2,1,0:T(8,128)}, u32[]{:S(2)}) copy-start(f32[1,256,768]{2,1,0:T(8,128)} %copy-done.62) | copy-start | bytes 2359300
  308.8 149.0 %all-reduce.30.cloned.1.call-start = ((), (), s32[]{:S(2)}) async-start(), calls=%async_computation.11 | async-start | bytes 1572864 | tf_op jit(solution)/shard_map/psum | solution.py:211
  372.6 5.3 collective-permute-start.1
  375.6 84.5 %copy-start.17 = (f32[1,256,768]{2,1,0:T(8,128)}, f32[1,256,768]{2,1,0:T(8,128)S(1)}, u32[]{:S(2)}) copy-start(f32[1,256,768]{2,1,0:T(8,128)S(1)} %get-tuple-element.126) | copy-start | bytes 2359300
  410.5 103.4 %all-reduce.32.cloned.1.call-start = ((), (), s32[]{:S(2)}) async-start(), calls=%async_computation.12 | async-start | bytes 1572864 | tf_op jit(solution)/shard_map/psum | solution.py:211
  465.1 103.8 %all-reduce.34.cloned.1.call-start = ((), (), s32[]{:S(2)}) async-start(), calls=%async_computation.13 | async-start | bytes 1572864 | tf_op jit(solution)/shard_map/psum | solution.py:310
  520.0 48.9 %copy-start.23 = (f32[1,256,768]{2,1,0:T(8,128)S(1)}, f32[1,256,768]{2,1,0:T(8,128)}, u32[]{:S(2)}) copy-start(f32[1,256,768]{2,1,0:T(8,128)} %copy-done.22) | copy-start | bytes 2359300
  520.0 198.5 %all-reduce.36.cloned.1.call-start = ((), (), s32[]{:S(2)}) async-start(), calls=%async_computation.14 | async-start | bytes 1572864 | tf_op jit(solution)/shard_map/psum | solution.py:310
  611.7 53.9 %copy-start.55 = (bf16[2,1,256,768]{3,2,1,0:T(8,128)(2,1)S(1)}, bf16[2,1,256,768]{3,2,1,0:T(8,128)(2,1)}, u32[]{:S(2)}) copy-start(bf16[2,1,256,768]{3,2,1,0:T(8,128)(2,1)} %param.27) | copy-start | bytes 2359300
  643.9 21.6 %collective-permute-start.2 = (bf16[1,256,768]{2,1,0:T(8,128)(2,1)}, bf16[1,256,768]{2,1,0:T(8,128)(2,1)S(1)}, u32[]{:S(2)}, u32[]{:S(2)}) collective-permute-start(bf16[1,256,768]{2,1,0:T(8,128)(2,1)} %all-reduce.49), channel_id=1, source_target_pairs={{16,0},{17,1},{18,2},{19,3},{20,4},{21,5},{22,6},{23,7},{24,8},{25... | collective-permute-start | bytes 1179656 | tf_op jit(solution)/shard_map/ppermute | solution.py:22
  666.9 51.6 %copy-start.373 = (f32[256]{0:T(256)}, f32[256]{0:T(256)S(1)}, u32[]{:S(2)}) copy-start(f32[256]{0:T(256)S(1)} %negate_multiply_fusion.8) | copy-start | bytes 3076
  669.7 48.8 %copy-start.81 = (f32[1,256,768]{2,1,0:T(8,128)S(1)}, f32[1,256,768]{2,1,0:T(8,128)}, u32[]{:S(2)}) copy-start(f32[1,256,768]{2,1,0:T(8,128)} %copy-done.80) | copy-start | bytes 2359300
  669.7 48.8 %copy-start.295 = (f32[256]{0:T(256)S(1)}, f32[256]{0:T(256)}, u32[]{:S(2)}) copy-start(f32[256]{0:T(256)} %copy-done.294) | copy-start | bytes 3076
  669.7 48.8 %copy-start.306 = (f32[256]{0:T(256)S(1)}, f32[256]{0:T(256)}, u32[]{:S(2)}) copy-start(f32[256]{0:T(256)} %copy-done.305) | copy-start | bytes 3076
  669.7 195.3 %all-reduce.38.cloned.1.call-start = ((), (), s32[]{:S(2)}) async-start(), calls=%async_computation.15 | async-start | bytes 1572864 | tf_op jit(solution)/shard_map/psum | solution.py:310
  759.3 50.4 %copy-start.207 = (bf16[1,256,192]{1,2,0:T(8,128)(2,1)S(1)}, bf16[1,256,192]{1,2,0:T(8,128)(2,1)}, u32[]{:S(2)}) copy-start(bf16[1,256,192]{1,2,0:T(8,128)(2,1)} %copy.124) | copy-start | bytes 294916
  759.3 52.7 %copy-start.25 = (f32[1,256,768]{2,1,0:T(8,128)S(1)}, f32[1,256,768]{2,1,0:T(8,128)}, u32[]{:S(2)}) copy-start(f32[1,256,768]{2,1,0:T(8,128)} %copy-done.24) | copy-start | bytes 2359300
  759.3 52.7 %copy-start.56 = (bf16[2,1,256,768]{3,2,1,0:T(8,128)(2,1)S(1)}, bf16[2,1,256,768]{3,2,1,0:T(8,128)(2,1)}, u32[]{:S(2)}) copy-start(bf16[2,1,256,768]{3,2,1,0:T(8,128)(2,1)} %param.27) | copy-start | bytes 2359300
  759.3 52.7 %copy-start.300 = (f32[256]{0:T(256)S(1)}, f32[256]{0:T(256)}, u32[]{:S(2)}) copy-start(f32[256]{0:T(256)} %copy-done.299) | copy-start | bytes 3076
  759.3 52.7 %copy-start.337 = (f32[256]{0:T(256)S(1)}, f32[256]{0:T(256)}, u32[]{:S(2)}) copy-start(f32[256]{0:T(256)} %copy-done.336) | copy-start | bytes 3076
  791.6 20.4 %collective-permute-start.3 = (bf16[1,256,768]{2,1,0:T(8,128)(2,1)}, bf16[1,256,768]{2,1,0:T(8,128)(2,1)S(1)}, u32[]{:S(2)}, u32[]{:S(2)}) collective-permute-start(bf16[1,256,768]{2,1,0:T(8,128)(2,1)} %all-reduce.50), channel_id=1, source_target_pairs={{16,0},{17,1},{18,2},{19,3},{20,4},{21,5},{22,6},{23,7},{24,8},{25... | collective-permute-start | bytes 1179656 | tf_op jit(solution)/shard_map/ppermute | solution.py:22
  813.4 51.6 %copy-start.350 = (f32[256]{0:T(256)}, f32[256]{0:T(256)S(1)}, u32[]{:S(2)}) copy-start(f32[256]{0:T(256)S(1)} %negate_multiply_fusion.5) | copy-start | bytes 3076
  816.2 200.8 %all-reduce.44.cloned.1.call-start = ((), (), s32[]{:S(2)}) async-start(), calls=%async_computation.26 | async-start | bytes 4718592 | tf_op jit(solution)/shard_map/psum | solution.py:336
  873.2 61.5 %copy-start.209 = (bf16[256,192]{0,1:T(8,128)(2,1)S(1)}, bf16[256,192]{0,1:T(8,128)(2,1)}, u32[]{:S(2)}) copy-start(bf16[256,192]{0,1:T(8,128)(2,1)} %copy-done.208) | copy-start | bytes 294916
  876.0 339.4 %reduce-scatter.29.cloned.1.call-start = ((), (), s32[]{:S(2)}) async-start(), calls=%async_computation.19 | async-start | bytes 491520
  876.2 75.1 %copy-start.321 = (f32[768]{0:T(1024)S(1)}, f32[768]{0:T(1024)}, u32[]{:S(2)}) copy-start(f32[768]{0:T(1024)} %get-tuple-element.68) | copy-start | bytes 9220
  876.2 75.7 %copy-start.74 = (f32[1,256,768]{2,1,0:T(8,128)S(1)}, f32[1,256,768]{2,1,0:T(8,128)}, u32[]{:S(2)}) copy-start(f32[1,256,768]{2,1,0:T(8,128)} %copy-done.73) | copy-start | bytes 2359300
  876.2 75.7 %copy-start.138 = (bf16[256,768]{1,0:T(8,128)(2,1)S(1)}, bf16[256,768]{1,0:T(8,128)(2,1)}, u32[]{:S(2)}) copy-start(bf16[256,768]{1,0:T(8,128)(2,1)} %copy-done.137) | copy-start | bytes 1179652
  876.3 75.7 %copy-start.372 = (f32[256]{0:T(256)S(1)}, f32[256]{0:T(256)}, u32[]{:S(2)}) copy-start(f32[256]{0:T(256)} %copy-done.371) | copy-start | bytes 3076
  961.0 274.7 %reduce-scatter.37.cloned.1.call-start = ((), (), s32[]{:S(2)}) async-start(), calls=%async_computation.23 | async-start | bytes 884736
  965.2 272.0 %all-reduce.40.cloned.1.call-start = ((), (), s32[]{:S(2)}) async-start(), calls=%async_computation.24 | async-start | bytes 4718592
  981.9 257.8 %reduce-scatter.31.cloned.1.call-start = ((), (), s32[]{:S(2)}) async-start(), calls=%async_computation.20 | async-start | bytes 491520
  1036.2 205.1 %reduce-scatter.33.cloned.1.call-start = ((), (), s32[]{:S(2)}) async-start(), calls=%async_computation.21 | async-start | bytes 491520
  1039.3 203.9 %reduce-scatter.27.cloned.1.call-start = ((), (), s32[]{:S(2)}) async-start(), calls=%async_computation.18 | async-start | bytes 983040
  1043.2 201.8 %reduce-scatter.35.cloned.1.call-start = ((), (), s32[]{:S(2)}) async-start(), calls=%async_computation.22 | async-start | bytes 2211840
  1056.1 261.8 %all-reduce.42.cloned.1.call-start = ((), (), s32[]{:S(2)}) async-start(), calls=%async_computation.25 | async-start | bytes 4718592 | tf_op jit(solution)/shard_map/psum | solution.py:367
  1060.9 69.4 %copy-start.171 = (bf16[256,192]{0,1:T(8,128)(2,1)}, bf16[256,192]{0,1:T(8,128)(2,1)S(1)}, u32[]{:S(2)}) copy-start(bf16[256,192]{0,1:T(8,128)(2,1)S(1)} %convolution_convert_fusion.6) | copy-start | bytes 294916
  1077.3 69.4 %copy-start.206 = (bf16[1024,192]{0,1:T(8,128)(2,1)}, bf16[1024,192]{0,1:T(8,128)(2,1)S(1)}, u32[]{:S(2)}) copy-start(bf16[1024,192]{0,1:T(8,128)(2,1)S(1)} %all-gather.8) | copy-start | bytes 1179652
  1198.1 163.6 %reduce-scatter.25.cloned.1.call-start = ((), (), s32[]{:S(2)}) async-start(), calls=%async_computation.17 | async-start | bytes 2457600
  1207.7 204.3 %reduce-scatter.23.cloned.1.call-start = ((), (), s32[]{:S(2)}) async-start(), calls=%async_computation.16 | async-start | bytes 2949120 | tf_op jit(solution)/shard_map/reduce_scatter | solution.py:412
  1215.4 102.7 %copy-start.174 = (bf16[1,2,1,256,768]{4,3,1,2,0:T(8,128)(2,1)}, bf16[1,2,1,256,768]{4,3,1,2,0:T(8,128)(2,1)S(1)}, u32[]{:S(2)}) copy-start(bf16[1,2,1,256,768]{4,3,1,2,0:T(8,128)(2,1)S(1)} %fusion.218) | copy-start | bytes 2359300
  1237.3 80.8 %copy-start.34 = (f32[1,256,768]{2,1,0:T(8,128)S(1)}, f32[1,256,768]{2,1,0:T(8,128)}, u32[]{:S(2)}) copy-start(f32[1,256,768]{2,1,0:T(8,128)} %copy-done.33) | copy-start | bytes 2359300
  1237.3 80.8 %copy-start.344 = (f32[256]{0:T(256)S(1)}, f32[256]{0:T(256)}, u32[]{:S(2)}) copy-start(f32[256]{0:T(256)} %copy-done.342) | copy-start | bytes 3076
  1242.4 77.2 %copy-start.32 = (f32[1,256,768]{2,1,0:T(8,128)S(1)}, f32[1,256,768]{2,1,0:T(8,128)}, u32[]{:S(2)}) copy-start(f32[1,256,768]{2,1,0:T(8,128)} %get-tuple-element.207) | copy-start | bytes 2359300
  1242.4 77.2 %copy-start.341 = (f32[256]{0:T(256)S(1)}, f32[256]{0:T(256)}, u32[]{:S(2)}) copy-start(f32[256]{0:T(256)} %negate_multiply_fusion.6) | copy-start | bytes 3076
  1319.8 92.2 %copy-start.1 = (bf16[1,768,768]{2,1,0:T(8,128)(2,1)S(1)}, bf16[1,768,768]{2,1,0:T(8,128)(2,1)}, u32[]{:S(2)}) copy-start(bf16[1,768,768]{2,1,0:T(8,128)(2,1)} %param.18) | copy-start | bytes 3538948
  1320.1 91.9 %copy-start.173 = (bf16[1,2,1,256,768]{4,3,2,1,0:T(8,128)(2,1)}, bf16[1,2,1,256,768]{4,3,2,1,0:T(8,128)(2,1)S(1)}, u32[]{:S(2)}) copy-start(bf16[1,2,1,256,768]{4,3,2,1,0:T(8,128)(2,1)S(1)} %fusion.227) | copy-start | bytes 2359300
  (352 other events, 3210.5 us)
Sparse Core Ops, SparseCore 0:
  42.8 48.0 all-reduce.23
  99.5 48.3 all-reduce.25
  155.6 61.0 all-reduce.47
  254.0 47.2 all-reduce.27
  309.0 61.0 all-reduce.45
  410.7 47.0 all-reduce.29
  465.2 48.7 all-reduce.31
  520.1 48.7 all-reduce.33
  669.8 48.6 all-reduce.35
  816.3 48.6 all-reduce.37
  876.1 74.4 all-reduce.43
  961.1 22.1 reduce-scatter.28
  985.6 33.1 reduce-scatter.36
  1021.1 103.5 all-reduce.39
  1127.0 18.8 reduce-scatter.30
  1148.0 19.5 reduce-scatter.32
  1169.8 21.7 reduce-scatter.26
  1193.9 47.1 reduce-scatter.34
  1244.5 73.4 all-reduce.41
  1320.3 41.4 reduce-scatter.24
  1364.7 47.2 reduce-scatter.22
where the time goes:
time: 1430 us; the launch traced here: 1420 us
  blocking collectives  550 us (38%)
  waiting for transfers between devices  463 us (32%)
  matrix products  193 us (13%)
  local copies, waits for them, and re-layouts  120 us (8%)
  other arithmetic  63.4 us (4%)
  between operations  20.7 us (1%)
    psum x7, waiting for transfers between devices, head_total(): return lax.psum(partial_value, 'tp')  242 us
    all_gather x6, blocking collectives, share_keys(): return lax.all_gather(local_kv, 'seq', axis=1, tiled=True)  116 us
    all_gather x6, blocking collectives, key_gradients(): grad_piece = lax.all_gather(grad_mixture, 'seq', axis=1, tiled=True)  97.1 us
    all_gather x6, blocking collectives, key_gradients(): lax.all_gather(for_sending(queries), 'seq', axis=1, tiled=True)  94.7 us
    all_gather x6, blocking collectives, key_gradients(): lax.all_gather(row_inner, 'seq', axis=2, tiled=True)  83.1 us
    all_gather x6, blocking collectives, key_gradients(): lax.all_gather(log_total, 'seq', axis=2, tiled=True)  82.4 us
    psum x1, waiting for transfers between devices, on_device(): lax.psum(linear_back(grad_queries_bf, qkv_weight[0]) + linear_back(grad_k...  71.1 us
    psum x3, waiting for transfers between devices, on_device(): lax.psum(linear_back(grad_before, weight_in), 'tp')  60.6 us
  transfers between devices with their start and end apart: 25, of which 12 were waited for; matrix products, arithmetic and copies ran while one was open for 17% of the time, Pallas kernels for 0%

commit v1 on v0

v1 whole, which is shorter than its diff:
```python
import math

import jax
import jax.numpy as jnp
from jax import lax
from jax.experimental import pallas as pl
from jax.experimental.pallas import tpu as pltpu
from jax.sharding import PartitionSpec as P

HEAD_DIM = 64
EPSILON = 1e-05
MASKED_OUT = -1e30
SCALE = 1.0 / math.sqrt(HEAD_DIM)
F32 = jnp.float32
BF16 = jnp.bfloat16
MIB = 1 << 20

GAIN_ATT, GAIN_END, SHIFT_ATT, SHIFT_END, BIAS_OUT, BIAS_IN = range(6)


def shape(dims, kind):
    return jax.ShapeDtypeStruct(dims, kind)


def dot(left, right, left_dim=1, right_dim=0):
    return lax.dot_general(
        left, right, (((left_dim,), (right_dim,)), ((), ())), preferred_element_type=F32
    )


def call(name, body, outs, *args, flops=0, vmem=24 * MIB):
    def kernel(*refs):
        body(refs[: len(args)], refs[len(args) :])

    moved = sum(math.prod(a.shape) * a.dtype.itemsize for a in (*args, *outs))
    return pl.pallas_call(
        kernel,
        out_shape=outs,
        in_specs=[pl.BlockSpec(memory_space=pltpu.VMEM)] * len(args),
        out_specs=[pl.BlockSpec(memory_space=pltpu.VMEM)] * len(outs),
        compiler_params=pltpu.CompilerParams(vmem_limit_bytes=vmem),
        cost_estimate=pl.CostEstimate(flops=flops, bytes_accessed=moved, transcendentals=0),
        name=name,
    )(*args)


def swap_cores(block):
    return lax.ppermute(block, "section", [(0, 1), (1, 0)])


def xor_perm(block, axis, bits):
    return lax.ppermute(block, axis, [(i, i ^ bits) for i in range(lax.axis_size(axis))])


def scatter_tp(pieces):
    order = sorted(range(1, len(pieces) + 1), key=lambda i: -bin(i).count("1"))
    got = {i: xor_perm(pieces[i - 1], "tp", i) for i in order}
    return [got[i] for i in range(1, len(pieces) + 1)]


def gather_tp(block):
    return [block] + scatter_tp([block] * (lax.axis_size("tp") - 1))


def normalized(values):
    centred = values - jnp.mean(values, axis=-1, keepdims=True)
    spread = jnp.mean(centred * centred, axis=-1, keepdims=True)
    inverse = lax.rsqrt(spread + EPSILON)
    return centred * inverse, inverse


def norm_back(values, gain, upstream):
    unit, inverse = normalized(values)
    scaled = gain * upstream
    grad = (
        scaled
        - jnp.mean(scaled, axis=-1, keepdims=True)
        - unit * jnp.mean(scaled * unit, axis=-1, keepdims=True)
    ) * inverse
    gain_grad = jnp.sum(upstream * unit, axis=0, keepdims=True)
    shift_grad = jnp.sum(upstream, axis=0, keepdims=True)
    return grad, gain_grad, shift_grad


def put_rows(ref, rows):
    width = ref.shape[1]
    ref[...] = jnp.concatenate(rows + [jnp.zeros((8 - len(rows), width), F32)], axis=0)


def summed(own, received):
    total = own[...]
    for ref in received:
        total = total + ref[...].astype(F32)
    return total


def norm_forward(name, own, received, residual, vectors, rows, bias_row=None):
    count = len(received)

    def body(ins, outs):
        total = summed(ins[0], ins[1 : 1 + count]) + ins[1 + count][...].astype(F32)
        vec = ins[2 + count]
        if bias_row is not None:
            total = total + vec[bias_row : bias_row + 1, :]
        unit, _ = normalized(total)
        result = unit * vec[rows[0] : rows[0] + 1, :] + vec[rows[1] : rows[1] + 1, :]
        outs[0][...] = total
        outs[1][...] = result
        outs[2][...] = result.astype(BF16)

    kinds = [shape(own.shape, F32), shape(own.shape, F32), shape(own.shape, BF16)]
    return call(name, body, kinds, own, *received, residual, vectors)


def norm_backward(name, own, received, residual, values, vectors, row, round_first=False):
    count = len(received)
    args = [own, *received, values, vectors] + ([] if residual is None else [residual])

    def body(ins, outs):
        upstream = summed(ins[0], ins[1 : 1 + count])
        values_ref, vec = ins[1 + count], ins[2 + count]
        if residual is not None:
            upstream = upstream + ins[3 + count][...]
        if round_first:
            upstream = upstream.astype(BF16).astype(F32)
        grad, gain_grad, shift_grad = norm_back(values_ref[...], vec[row : row + 1, :], upstream)
        outs[0][...] = grad
        outs[1][...] = grad.astype(BF16)
        put_rows(outs[2], [gain_grad, shift_grad, jnp.sum(grad, axis=0, keepdims=True)])

    kinds = [shape(own.shape, F32), shape(own.shape, BF16), shape((8, own.shape[1]), F32)]
    return call(name, body, kinds, *args)


def norm_turn(name, own, received, residual, cotangent, vectors):
    count = len(received)

    def body(ins, outs):
        vec = ins[3 + count]
        total = summed(ins[0], ins[1 : 1 + count]) + ins[1 + count][...]
        total = total + vec[BIAS_OUT : BIAS_OUT + 1, :]
        unit, _ = normalized(total)
        gain = vec[GAIN_END : GAIN_END + 1, :]
        outs[0][...] = (unit * gain + vec[SHIFT_END : SHIFT_END + 1, :]).astype(BF16)
        upstream = ins[2 + count][...].astype(F32)
        grad, gain_grad, shift_grad = norm_back(total, gain, upstream)
        outs[1][...] = grad
        outs[2][...] = grad.astype(BF16)
        put_rows(outs[3], [gain_grad, shift_grad, jnp.sum(grad, axis=0, keepdims=True)])

    dims = own.shape
    kinds = [shape(dims, BF16), shape(dims, F32), shape(dims, BF16), shape((8, dims[1]), F32)]
    return call(name, body, kinds, own, *received, residual, cotangent, vectors)


def joined(refs):
    return jnp.concatenate([ref[...] for ref in refs], axis=0)


def store_pieces(refs, value):
    rows = refs[0].shape[0]
    for i, ref in enumerate(refs):
        ref[...] = value[i * rows : (i + 1) * rows].astype(ref.dtype)


def piece_kinds(tokens, width, count):
    rows = tokens // count
    return [shape((rows, width), F32)] + [shape((rows, width), BF16)] * (count - 1)


def project(name, pieces, weight, groups):
    count = len(pieces)
    tokens = sum(p.shape[0] for p in pieces)
    width = weight.shape[2]

    def body(ins, outs):
        values = joined(ins[:count])
        for out, group in zip(outs, groups):
            for at, i in enumerate(group):
                out[:, at * width : (at + 1) * width] = dot(values, ins[count][i]).astype(BF16)

    kinds = [shape((tokens, width * len(g)), BF16) for g in groups]
    return call(name, body, kinds, *pieces, weight)


def project_back(name, grads, weight, picks, pieces):
    tokens = grads[0].shape[0]

    def body(ins, outs):
        total = 0.0
        for ref, (i, start, size) in zip(ins, picks):
            total = total + dot(ref[:, start : start + size], ins[len(grads)][i], 1, 1)
        store_pieces(outs, total)

    return call(name, body, piece_kinds(tokens, weight.shape[1], pieces), *grads, weight)


HALF_ROOT = 0.5**0.5
DENSITY = 1.0 / math.sqrt(2.0 * math.pi)


def feed_forward(name, pieces, weight_in, vectors, weight_out):
    count = len(pieces)
    tokens = sum(p.shape[0] for p in pieces)
    units, width = weight_out.shape
    step = 256

    def body(ins, outs):
        values = joined(ins[:count])
        win, vec, wout = ins[count : count + 3]
        total = 0.0
        for at in range(0, units, step):
            before = dot(values, win[:, at : at + step]) + vec[BIAS_IN : BIAS_IN + 1, at : at + step]
            outs[0][:, at : at + step] = before
            active = (0.5 * before * (1.0 + lax.erf(before * HALF_ROOT))).astype(BF16)
            outs[1][:, at : at + step] = active
            total = total + dot(active, wout[at : at + step, :])
        store_pieces(outs[2:], total)

    kinds = [shape((tokens, units), F32), shape((tokens, units), BF16)]
    kinds += piece_kinds(tokens, width, count)
    flops = 4 * tokens * units * width
    out = call(name, body, kinds, *pieces, weight_in, vectors, weight_out, flops=flops)
    return out[0], out[1], out[2:]


def feed_backward(name, pieces, before, weight_in, weight_out):
    count = len(pieces)
    tokens = sum(p.shape[0] for p in pieces)
    units, width = weight_out.shape
    step = 256

    def body(ins, outs):
        values = joined(ins[:count])
        before_ref, win, wout = ins[count : count + 3]
        total = 0.0
        sums = []
        for at in range(0, units, step):
            grad_active = dot(values, wout[at : at + step, :], 1, 1)
            u = before_ref[:, at : at + step]
            slope = 0.5 * (1.0 + lax.erf(u * HALF_ROOT)) + u * (DENSITY * jnp.exp(-0.5 * u * u))
            grad = (slope * grad_active).astype(BF16)
            outs[0][:, at : at + step] = grad
            sums.append(jnp.sum(grad.astype(F32), axis=0, keepdims=True))
            total = total + dot(grad, win[:, at : at + step], 1, 1)
        put_rows(outs[1], [jnp.concatenate(sums, axis=1)])
        store_pieces(outs[2:], total)

    kinds = [shape((tokens, units), BF16), shape((8, units), F32)]
    kinds += piece_kinds(tokens, width, count)
    flops = 4 * tokens * units * width
    out = call(name, body, kinds, *pieces, before, weight_in, weight_out, flops=flops)
    return out[0], out[1], out[2:]


def head_block(flipped, head, heads):
    tokens = flipped.shape[1]
    parts = []
    if head:
        parts.append(jnp.zeros((HEAD_DIM * head, tokens), flipped.dtype))
    parts.append(flipped[HEAD_DIM * head : HEAD_DIM * (head + 1)])
    if head < heads - 1:
        parts.append(jnp.zeros((HEAD_DIM * (heads - 1 - head), tokens), flipped.dtype))
    return jnp.concatenate(parts, axis=0) if len(parts) > 1 else parts[0]


def allowed_keys(ins, piece, tokens, group, span, causal):
    at = piece * tokens + group * span
    allowed = ins[1][at : at + span, :] == ins[0][:, group * span : (group + 1) * span]
    if causal:
        earlier = ins[3][at : at + span, :] <= ins[2][:, group * span : (group + 1) * span]
        allowed = allowed & earlier
    return allowed


def attend(name, queries, pieces, marks, causal, weight_out, rows, tp):
    tokens, width = queries.shape
    span = tokens // rows
    heads = width // HEAD_DIM
    count = len(pieces)

    def body(ins, outs):
        wout, mark = ins[1], ins[2 : 2 + len(marks)]
        kv = ins[2 + len(marks) :]
        mixed = []
        for group in range(rows):
            part = slice(group * span, (group + 1) * span)
            flipped = (ins[0][part, :] * BF16(SCALE)).T
            value_rows = [ref[part, width:].T for ref in kv]
            masks = [allowed_keys(mark, p, tokens, group, span, causal) for p in range(count)]
            mixtures, logs = [], []
            for head in range(heads):
                block = head_block(flipped, head, heads)
                scores = [
                    jnp.where(masks[p], dot(kv[p][part, :width], block), MASKED_OUT)
                    for p in range(count)
                ]
                largest = scores[0]
                for s in scores[1:]:
                    largest = jnp.maximum(largest, s)
                largest = jnp.max(largest, axis=0, keepdims=True)
                total, mixture = 0.0, 0.0
                for p in range(count):
                    e = jnp.exp(scores[p] - largest)
                    total = total + jnp.sum(e, axis=0, keepdims=True)
                    own = value_rows[p][HEAD_DIM * head : HEAD_DIM * (head + 1)]
                    mixture = mixture + dot(own, e.astype(BF16))
                mixtures.append(mixture * (1.0 / total))
                logs.append(largest + jnp.log(total))
            logs.append(jnp.zeros((8 - heads, span), F32))
            outs[1][group] = jnp.concatenate(logs, axis=0)
            mixed.append(jnp.concatenate(mixtures, axis=0).T.astype(BF16))
        result = jnp.concatenate(mixed, axis=0) if rows > 1 else mixed[0]
        outs[0][...] = result
        store_pieces(outs[2:], dot(result, wout[...]))

    kinds = [shape((tokens, width), BF16), shape((rows, 8, span), F32)]
    kinds += piece_kinds(tokens, weight_out.shape[1], tp)
    flops = 4 * tokens * span * count * heads * 256
    out = call(name, body, kinds, queries, weight_out, *marks, *pieces, flops=flops)
    return out[0], out[1], out[2:]


def attend_back(name, upstream, weight_out, queries, pieces, marks, causal, logs, rows, near):
    tokens, width = queries.shape
    span = tokens // rows
    heads = width // HEAD_DIM
    count = len(pieces)
    first = len(upstream)

    def body(ins, outs):
        wout = ins[first][...]
        mark = ins[first + 3 : first + 3 + len(marks)]
        kv = ins[first + 3 + len(marks) :]
        all_grad = joined(ins[:first])
        grad_rows = dot(all_grad, wout, 1, 1).astype(BF16)
        for group in range(rows):
            part = slice(group * span, (group + 1) * span)
            grad = grad_rows[part]
            grad_flipped = dot(wout, all_grad[part], 1, 1).astype(BF16)
            scaled = ins[first + 1][part, :] * BF16(SCALE)
            flipped = scaled.T
            key_rows = [ref[part, :width].T for ref in kv]
            masks = [allowed_keys(mark, p, tokens, group, span, causal) for p in range(count)]
            lane = lax.broadcasted_iota(jnp.int32, (span, width), 1)
            key_grads, value_grads, query_grads = [0.0] * count, [0.0] * count, []
            for head in range(heads):
                mine = (lane >= HEAD_DIM * head) & (lane < HEAD_DIM * (head + 1))
                block = head_block(flipped, head, heads)
                grad_block = head_block(grad_flipped, head, heads)
                query_part = jnp.where(mine, scaled, BF16(0.0))
                grad_part = jnp.where(mine, grad, BF16(0.0))
                log_row = ins[first + 2][group, head : head + 1, :]
                weights, weight_grads, inner = [], [], 0.0
                for p in range(count):
                    s = jnp.where(masks[p], dot(kv[p][part, :width], block), MASKED_OUT)
                    w = jnp.exp(s - log_row)
                    g = dot(kv[p][part, width:], grad_block)
                    inner = inner + jnp.sum(w * g, axis=0, keepdims=True)
                    value_grads[p] = value_grads[p] + dot(w.astype(BF16), grad_part)
                    weights.append(w)
                    weight_grads.append(g)
                query_grad = 0.0
                for p in range(count):
                    score_grad = (weights[p] * (weight_grads[p] - inner)).astype(BF16)
                    key_grads[p] = key_grads[p] + dot(score_grad, query_part)
                    own = key_rows[p][HEAD_DIM * head : HEAD_DIM * (head + 1)]
                    query_grad = query_grad + dot(own, score_grad)
                query_grads.append(query_grad)
            outs[0][part, :] = (jnp.concatenate(query_grads, axis=0) * SCALE).T.astype(BF16)
            for p in range(count):
                out, at = (outs[1], p) if p < near else (outs[2], p - near)
                at = slice(at * tokens + group * span, at * tokens + (group + 1) * span)
                out[at, :width] = key_grads[p].astype(out.dtype)
                out[at, width:] = value_grads[p].astype(out.dtype)

    kinds = [
        shape((tokens, width), BF16),
        shape((near * tokens, 2 * width), F32),
        shape(((count - near) * tokens, 2 * width), BF16),
    ]
    flops = 10 * tokens * span * count * heads * 256
    args = (*upstream, weight_out, queries, logs, *marks, *pieces)
    return call(name, body, kinds, *args, flops=flops)


def weight_partials(name, pairs, where, order, per):
    tokens, width = pairs[0][0].shape
    columns = sum(right.shape[1] for _, right in pairs)
    lefts, rights = [], []
    for left, right in pairs:
        lefts.append(left)
        rights.append(right)
    count = len(order)
    align = 16 if per % 16 == 0 else 8

    def kernel(where_ref, *refs):
        ins, out, turned = refs[: 2 * len(pairs)], refs[2 * len(pairs)], refs[2 * len(pairs) + 1 :]
        at = 0
        for i in range(len(pairs)):
            right = ins[len(pairs) + i][...]
            held = turned[i]
            held[...] = ins[i][...].astype(held.dtype).T
            for k in range(count):
                start = pl.multiple_of(where_ref[k] * per, align)
                got = dot(held[pl.ds(start, per), :].astype(BF16), right)
                out[k * per : (k + 1) * per, at : at + right.shape[1]] = got.astype(BF16)
            at += right.shape[1]

    moved = sum(math.prod(a.shape) * 2 for a in (*lefts, *rights)) + count * per * columns * 2
    return pl.pallas_call(
        kernel,
        out_shape=shape((count * per, columns), BF16),
        in_specs=[pl.BlockSpec(memory_space=pltpu.SMEM)]
        + [pl.BlockSpec(memory_space=pltpu.VMEM)] * (2 * len(pairs)),
        out_specs=pl.BlockSpec(memory_space=pltpu.VMEM),
        scratch_shapes=[pltpu.VMEM((width, tokens), BF16 if align == 16 else F32)] * len(pairs),
        compiler_params=pltpu.CompilerParams(vmem_limit_bytes=24 * MIB),
        cost_estimate=pl.CostEstimate(
            flops=2 * tokens * count * per * columns, bytes_accessed=moved, transcendentals=0
        ),
        name=name,
    )(where, *lefts, *rights)


def added(left, right, kind):
    return (left.astype(F32) + right.astype(F32)).astype(kind)


def on_device(
    hidden,
    segments,
    self_qkv,
    self_out,
    ffn_in,
    ffn_in_bias,
    ffn_out,
    norm_gains,
    norm_shifts,
    cross_qkv,
    cross_out,
    cross_gain,
    cross_shift,
    cotangent,
):
    section, seq, tp = (lax.axis_index(a) for a in ("section", "seq", "tp"))
    n_seq, n_tp = lax.axis_size("seq"), lax.axis_size("tp")
    half = n_seq // 2
    low_half = seq < half
    on_first = section == 0
    settled = on_first == low_half
    rows, span, width = hidden.shape[2:]
    tokens = rows * span
    sub = tokens // n_tp
    micro = seq // half

    both = ("section", "seq")
    low = range(half)
    to_encoder = [(z, z + half) for z in low] + [(z + half, n_seq + z) for z in low]
    to_decoder = [(n_seq + z, z + half) for z in low] + [(n_seq + z + half, n_seq + z) for z in low]
    across = [(z + half, n_seq + z + half) for z in low] + [(n_seq + z, z) for z in low]

    def spread(near, far):
        far_enc = lax.ppermute(far, both, to_encoder)
        core = lax.ppermute(near, both, across)
        far_dec = lax.ppermute(far, both, to_decoder)
        enc = jnp.where(settled, jnp.where(on_first, near, core), far_enc)
        dec = jnp.where(settled, jnp.where(on_first, core, near), far_dec)
        return enc, dec

    def collect(enc, dec):
        far_enc = lax.ppermute(enc, both, [(b, a) for a, b in to_encoder])
        far_dec = lax.ppermute(dec, both, [(b, a) for a, b in to_decoder])
        core = lax.ppermute(jnp.where(on_first, dec, enc), both, [(b, a) for a, b in across])
        near = jnp.where(settled, jnp.where(on_first, enc, dec), core)
        far = jnp.where(on_first, far_enc, far_dec)
        return jnp.stack([jnp.where(low_half, near, far), jnp.where(low_half, far, near)])

    def relative(block):
        cut = block.reshape(n_tp, sub, *block.shape[1:])
        return jnp.concatenate(
            [lax.dynamic_index_in_dim(cut, tp ^ i, 0, keepdims=False) for i in range(n_tp)]
        )

    both_micro = hidden[0].reshape(2, tokens, width)
    near = jnp.where(low_half, both_micro[0], both_micro[1])
    far = jnp.where(low_half, both_micro[1], both_micro[0])
    input_enc, input_dec = spread(near, far)
    input_enc, input_dec = relative(input_enc), relative(input_dec)

    vectors = jnp.concatenate(
        [norm_gains[0], norm_shifts[0], ffn_in_bias[0], jnp.zeros((2, width), F32)]
    )

    def layers(own):
        other = swap_cores(own)
        return jnp.where(on_first, own, other), jnp.where(on_first, other, own)

    qkv_enc, qkv_dec = layers(self_qkv[0])
    vec_enc, vec_dec = layers(vectors)
    out_enc, out_dec = layers(self_out[0])
    win_enc, win_dec = layers(ffn_in[0])
    wout_enc, wout_dec = layers(ffn_out[0])
    vec_cross = jnp.concatenate(
        [cross_gain[None], cross_gain[None], cross_shift[None], jnp.zeros((5, width), F32)]
    )

    ids = lax.dynamic_index_in_dim(segments, micro, 1, keepdims=False)
    own_z = seq % half

    def chunk_marks(at):
        cut = lax.dynamic_slice_in_dim(ids, at * span, span, 2).reshape(2, tokens)
        place = jnp.broadcast_to(at * span + jnp.arange(span), (rows, span)).reshape(1, tokens)
        return relative(jnp.concatenate([cut, place]).T)

    offsets = [(dc, dz) for dc in range(2) for dz in range(half)]
    key_marks = jnp.concatenate(
        [chunk_marks((section ^ dc) * half + (own_z ^ dz)) for dc, dz in offsets]
    )
    query_marks = key_marks[:tokens].T
    key_enc, key_dec, key_place = (key_marks[:, i : i + 1] for i in range(3))
    query_enc, query_dec, query_place = (query_marks[i : i + 1] for i in range(3))
    marks_enc = (query_enc, key_enc)
    marks_dec = (query_dec, key_dec, query_place, key_place)
    marks_cross = (query_dec, key_enc)

    def share(own):
        mine = [own] + [xor_perm(own, "seq", dz) for dz in range(1, half)]
        return mine + [swap_cores(block) for block in mine]

    def settle(mine, theirs):
        total = mine + swap_cores(theirs).astype(F32)
        sent = [
            xor_perm(total[dz * tokens : (dz + 1) * tokens].astype(BF16), "seq", dz)
            for dz in range(1, half)
        ]
        own = total[:tokens]
        for block in sent:
            own = own + block.astype(F32)
        return own.astype(BF16)

    q_enc, kv_enc = project("qkv_enc", [input_enc], qkv_enc, [(0,), (1, 2)])
    all_enc = share(kv_enc)
    a_enc, log_enc, part = attend(
        "attend_enc", q_enc, all_enc, marks_enc, False, out_enc, rows, n_tp
    )
    z1_enc, h1_enc, h1b_enc = norm_forward(
        "norm_att_enc", part[0], scatter_tp(part[1:]), input_enc[:sub], vec_enc,
        (GAIN_ATT, SHIFT_ATT),
    )
    h1_pieces_enc = gather_tp(h1b_enc)

    q_dec, kv_dec = project("qkv_dec", [input_dec], qkv_dec, [(0,), (1, 2)])
    all_dec = share(kv_dec)
    a_dec, log_dec, part = attend(
        "attend_dec", q_dec, all_dec, marks_dec, True, out_dec, rows, n_tp
    )
    z1_dec, h1_dec, h1b_dec = norm_forward(
        "norm_att_dec", part[0], scatter_tp(part[1:]), input_dec[:sub], vec_dec,
        (GAIN_ATT, SHIFT_ATT),
    )
    h1_pieces_dec = gather_tp(h1b_dec)
    (q_cross,) = project("q_cross", h1_pieces_dec, cross_qkv, [(0,)])

    u_enc, g_enc, part = feed_forward("ffn_enc", h1_pieces_enc, win_enc, vec_enc, wout_enc)
    z2_enc, _, memory = norm_forward(
        "norm_end_enc", part[0], scatter_tp(part[1:]), h1_enc, vec_enc,
        (GAIN_END, SHIFT_END), BIAS_OUT,
    )
    memory_pieces = gather_tp(memory)

    (kv_cross,) = project("kv_cross", memory_pieces, cross_qkv, [(1, 2)])
    all_cross = share(kv_cross)
    a_cross, log_cross, part = attend(
        "attend_cross", q_cross, all_cross, marks_cross, False, cross_out, rows, n_tp
    )
    z_cross, h2, h2b = norm_forward(
        "norm_cross", part[0], scatter_tp(part[1:]), h1_dec, vec_cross, (GAIN_ATT, SHIFT_ATT)
    )
    h2_pieces = gather_tp(h2b)
    u_dec, g_dec, part = feed_forward("ffn_dec", h2_pieces, win_dec, vec_dec, wout_dec)

    cot = lax.dynamic_slice_in_dim(cotangent.reshape(2, tokens, width), tp * sub, sub, 1)
    cot_near = jnp.where(low_half, cot[0], cot[1])
    cot_far = jnp.where(low_half, cot[1], cot[0])
    cot_moved = lax.ppermute(
        cot_far, both, [(z, z + half) for z in low] + [(n_seq + z + half, n_seq + z) for z in low]
    )
    cot_own = jnp.where(settled, cot_near, cot_moved)

    decoded, dz2_dec, dz2b_dec, sums_end_dec = norm_turn(
        "norm_end_dec", part[0], scatter_tp(part[1:]), h2, cot_own, vec_dec
    )

    r_pieces_dec = gather_tp(dz2b_dec)
    du_dec, sums_in_dec, part = feed_backward("ffn_back_dec", r_pieces_dec, u_dec, win_dec, wout_dec)
    dzc, dzcb, sums_cross = norm_backward(
        "norm_back_cross", part[0], scatter_tp(part[1:]), dz2_dec, z_cross, vec_cross, GAIN_ATT
    )
    dzc_pieces = gather_tp(dzcb)

    dq_cross, near_kv, far_kv = attend_back(
        "attend_back_cross", dzc_pieces, cross_out, q_cross, all_cross, marks_cross, False,
        log_cross, rows, half,
    )
    heads_width = q_cross.shape[1]
    dkv_cross = settle(near_kv, far_kv)
    part = project_back(
        "memory_back", [dkv_cross, dkv_cross], cross_qkv,
        [(1, 0, heads_width), (2, heads_width, heads_width)], n_tp,
    )
    dz2_enc, dz2b_enc, sums_end_enc = norm_backward(
        "norm_back_end_enc", part[0], scatter_tp(part[1:]), None, z2_enc, vec_enc, GAIN_END,
        round_first=True,
    )
    r_pieces_enc = gather_tp(dz2b_enc)

    du_enc, sums_in_enc, part = feed_backward("ffn_back_enc", r_pieces_enc, u_enc, win_enc, wout_enc)
    dz1_enc, dz1b_enc, sums_att_enc = norm_backward(
        "norm_back_att_enc", part[0], scatter_tp(part[1:]), dz2_enc, z1_enc, vec_enc, GAIN_ATT
    )
    dz1_pieces_enc = gather_tp(dz1b_enc)

    whole = [(0, 0, heads_width), (1, 0, heads_width), (2, heads_width, heads_width)]
    dq_enc, near_kv, far_kv = attend_back(
        "attend_back_enc", dz1_pieces_enc, out_enc, q_enc, all_enc, marks_enc, False,
        log_enc, rows, half,
    )
    dkv_enc = settle(near_kv, far_kv)
    part = project_back("input_back_enc", [dq_enc, dkv_enc, dkv_enc], qkv_enc, whole, n_tp)
    received = scatter_tp(part[1:])
    dx_enc = part[0] + dz1_enc
    for block in received:
        dx_enc = dx_enc + block.astype(F32)

    part = project_back("query_back", [dq_cross], cross_qkv, [(0, 0, heads_width)], n_tp)
    dz1_dec, dz1b_dec, sums_att_dec = norm_backward(
        "norm_back_att_dec", part[0], scatter_tp(part[1:]), dzc, z1_dec, vec_dec, GAIN_ATT
    )
    dz1_pieces_dec = gather_tp(dz1b_dec)
    dq_dec, near_kv, far_kv = attend_back(
        "attend_back_dec", dz1_pieces_dec, out_dec, q_dec, all_dec, marks_dec, True,
        log_dec, rows, half,
    )
    dkv_dec = settle(near_kv, far_kv)
    part = project_back("input_back_dec", [dq_dec, dkv_dec, dkv_dec], qkv_dec, whole, n_tp)
    received = scatter_tp(part[1:])
    dx_dec = part[0] + dz1_dec
    for block in received:
        dx_dec = dx_dec + block.astype(F32)

    def whole_chunk(enc, dec):
        found = collect(enc, dec)
        every = lax.all_gather(found, "tp", axis=1, tiled=True)
        return every.reshape(1, 2, rows, span, width)

    layer_out = whole_chunk(memory, decoded)
    grad_hidden = whole_chunk(dx_enc.astype(BF16), dx_dec.astype(BF16))

    bits = max(n_seq.bit_length() - 1, 0)
    order = sorted(range(n_seq), key=lambda r: int(format(r, f"0{bits}b")[::-1], 2))

    def along_seq(block, members):
        bit = 1
        while bit < n_seq:
            rows_now = block.shape[0] // 2
            route = [(s * n_seq + z, s * n_seq + (z ^ bit)) for s in members for z in range(n_seq)]
            got = lax.ppermute(block[rows_now:], both, route)
            bit *= 2
            block = added(block[:rows_now], got, F32 if bit == n_seq else BF16)
        return block

    def layer_grads(name, pairs, member):
        per = width // n_seq
        where = jnp.stack([seq ^ r for r in order]).astype(jnp.int32)
        block = weight_partials(name, pairs, where, order, per)
        other = lax.ppermute(block, "section", [(1 - member, member)])
        return along_seq(added(block, other, BF16), [member])

    ffn_grads, self_grads = [], []
    joined_h2 = jnp.concatenate(h2_pieces)
    joined_h1 = jnp.concatenate(h1_pieces_enc)
    joined_r_dec = jnp.concatenate(r_pieces_dec)
    joined_r_enc = jnp.concatenate(r_pieces_enc)
    joined_z_dec = jnp.concatenate(dz1_pieces_dec)
    joined_z_enc = jnp.concatenate(dz1_pieces_enc)
    dec_ffn = layer_grads("grad_ffn_dec", [(joined_h2, du_dec), (joined_r_dec, g_dec)], 1)

    per_cross = width // (2 * n_seq)
    cross_order = [(dc, r) for dc in range(2) for r in order]
    where = jnp.stack([(section ^ dc) * n_seq + (seq ^ r) for dc, r in cross_order])
    joined_h1_dec = jnp.concatenate(h1_pieces_dec)
    joined_memory = jnp.concatenate(memory_pieces)
    block = weight_partials(
        "grad_cross",
        [(joined_h1_dec, dq_cross), (joined_memory, dkv_cross), (jnp.concatenate(dzc_pieces), a_cross)],
        where.astype(jnp.int32), cross_order, per_cross,
    )
    mine = block.shape[0] // 2
    cross_sum = along_seq(added(block[:mine], swap_cores(block[mine:]), BF16), [0, 1])

    enc_ffn = layer_grads("grad_ffn_enc", [(joined_h1, du_enc), (joined_r_enc, g_enc)], 0)
    dec_self = layer_grads(
        "grad_self_dec", [(input_dec, dq_dec), (input_dec, dkv_dec), (joined_z_dec, a_dec)], 1
    )
    enc_self = layer_grads(
        "grad_self_enc", [(input_enc, dq_enc), (input_enc, dkv_enc), (joined_z_enc, a_enc)], 0
    )
    ffn_sum = jnp.where(on_first, enc_ffn, dec_ffn)
    self_sum = jnp.where(on_first, enc_self, dec_self)
    units = ffn_in.shape[2]

    def thirds(block):
        return jnp.stack([block[:, i * heads_width : (i + 1) * heads_width] for i in range(3)])

    mine_tp = (jnp.arange(n_tp) == tp)[:, None]
    table = jnp.concatenate(
        [
            sums_att_enc[:1], sums_end_enc[:1], sums_att_enc[1:2], sums_end_enc[1:3],
            sums_att_dec[:1], sums_end_dec[:1], sums_att_dec[1:2], sums_end_dec[1:3],
            sums_cross[:2],
            jnp.where(mine_tp, sums_in_enc[:1], 0.0),
            jnp.where(mine_tp, sums_in_dec[:1], 0.0),
        ]
    )
    table = lax.psum(table, ("section", "seq", "tp"))
    layer_rows = jnp.where(on_first, table[:5], table[5:10])
    bias_rows = jnp.where(on_first, table[12 : 12 + n_tp], table[12 + n_tp :])
    part_seq = lax.dynamic_slice_in_dim(layer_rows, seq * (width // n_seq), width // n_seq, 1)
    bias_row = lax.dynamic_index_in_dim(bias_rows, tp, 0)
    bias_part = lax.dynamic_slice_in_dim(bias_row, seq * (units // n_seq), units // n_seq, 1)
    cross_part = lax.dynamic_slice_in_dim(
        table[10:12], (section * n_seq + seq) * per_cross, per_cross, 1
    )

    return (
        layer_out,
        grad_hidden,
        thirds(self_sum)[None],
        self_sum[:, 3 * heads_width :].T[None],
        ffn_sum[:, :units][None],
        bias_part[None],
        ffn_sum[:, units:].T[None],
        part_seq[:2][None],
        part_seq[2:][None],
        thirds(cross_sum),
        cross_sum[:, 3 * heads_width :].T,
        cross_part[0],
        cross_part[1],
    )


def solution(mesh):
    return jax.shard_map(
        on_device,
        mesh=mesh,
        in_specs=(
            P("section", None, None, "seq", None),
            P(),
            P("section", None, None, "tp"),
            P("section", "tp", None),
            P("section", None, "tp"),
            P("section", "tp", None),
            P("section", "tp", None),
            P("section", None, None),
            P("section", None, None),
            P(None, None, "tp"),
            P("tp", None),
            P(),
            P(),
            P(None, None, "seq", None),
        ),
        out_specs=(
            P("section", None, None, "seq", None),
            P("section", None, None, "seq", None),
            P("section", None, "seq", "tp"),
            P("section", "tp", "seq"),
            P("section", "seq", "tp"),
            P("section", "tp", "seq"),
            P("section", "tp", "seq"),
            P("section", None, "seq"),
            P("section", None, "seq"),
            P(None, ("section", "seq"), "tp"),
            P("tp", ("section", "seq")),
            P(("section", "seq")),
            P(("section", "seq")),
        ),
        check_vma=False,
    )
```

time: 1430 us -> 469 us (0.33)
  blocking collectives: 550 us -> 68.1 us
  waiting for transfers between devices: 463 us -> 113 us
  matrix products: 193 us -> 0 us
  starting transfers between devices: 8.09 us -> 138 us
  local copies, waits for them, and re-layouts: 120 us -> 58.6 us
  Pallas kernels: 0 us -> 43.7 us
  other arithmetic: 63.4 us -> 35.2 us
  between operations: 20.7 us -> 2.99 us
    all_gather x30 -> x2, blocking collectives: 473 us -> 27.4 us  [whole_chunk(): every = lax.all_gather(found, 'tp', axis=1, tiled=True)]
    psum x12 -> x0, waiting for transfers between devices: 373 us -> none  [the longest x7 242 us: head_total(): return lax.psum(partial_value, 'tp')]
    dot_general x113 -> x0, matrix products: 193 us -> none  [the longest x23 35.8 us: linear_back(): jnp.einsum('rte,de->rtd', grads_in, weight, preferred_element_type=jnp.fl...]
    ppermute x4 -> x105, starting transfers between devices: 6.36 us -> 138 us  [the longest x66 78.9 us: xor_perm(): lax.ppermute(block, axis, [(i, i ^ bits) for i in range(lax.axis_size(axi...]
    ppermute x4 -> x105, waiting for transfers between devices: 0.01 us -> 113 us  [the longest x10 57.4 us: along_seq(): got = lax.ppermute(block[rows_now:], both, route)]
    reduce_sum x40 -> x0, other arithmetic: 48.2 us -> none  [the longest x16 19.1 us: norm_apply(): centred = values - jnp.mean(values, axis=-1, keepdims=True)]
    reduce_scatter x1 -> x0, waiting for transfers between devices: 48 us -> none  [on_device(): lax.psum_scatter(section_total[2], 'seq', scatter_dimension=1, tiled=True)]
    pallas_call x0 -> x32, Pallas kernels: none -> 43.7 us  [the longest x27 35.2 us: call(): pl.pallas_call(kernel, out_shape=outs, in_specs=[pl.BlockSpec(memory_spac...]
  transfers between devices with their start and end apart: 25 -> 105, of which waited for: 12 -> 42; matrix products, arithmetic and copies ran while one was open for 17% -> 14% of each run, Pallas kernels for 0% -> 9%
where the time goes in v1:
time: 469 us; the launch traced here: 460 us
  starting transfers between devices  138 us (29%)
  waiting for transfers between devices  113 us (24%)
  blocking collectives  68.1 us (15%)
  local copies, waits for them, and re-layouts  58.6 us (12%)
  Pallas kernels  43.7 us (9%)
  other arithmetic  35.2 us (8%)
    ppermute x66, starting transfers between devices, xor_perm(): lax.ppermute(block, axis, [(i, i ^ bits) for i in range(lax.axis_size(axi...  78.9 us
    ppermute x10, waiting for transfers between devices, along_seq(): got = lax.ppermute(block[rows_now:], both, route)  57.4 us
    ppermute x66, waiting for transfers between devices, xor_perm(): lax.ppermute(block, axis, [(i, i ^ bits) for i in range(lax.axis_size(axi...  50.7 us
    psum x1, blocking collectives, on_device(): table = lax.psum(table, ('section', 'seq', 'tp'))  40.6 us
    unnamed x264, local copies, waits for them, and re-layouts  35.4 us
    pallas_call x27, Pallas kernels, call(): pl.pallas_call(kernel, out_shape=outs, in_specs=[pl.BlockSpec(memory_spac...  35.2 us
    all_gather x2, blocking collectives, whole_chunk(): every = lax.all_gather(found, 'tp', axis=1, tiled=True)  27.4 us
    ppermute x10, starting transfers between devices, along_seq(): got = lax.ppermute(block[rows_now:], both, route)  17.8 us
  transfers between devices with their start and end apart: 105, of which 42 were waited for; matrix products, arithmetic and copies ran while one was open for 14% of the time, Pallas kernels for 9%

profile of v1, /device:TPU:0, one launch (start us, length us, event | category | flops | bytes accessed | tf_op | source)
XLA Modules:
  0.0 460.1 jit_solution(6839564774354547)
XLA Ops:
  1.9 6.0 %collective-permute-start.1 = (bf16[256,768]{1,0:T(8,128)(2,1)S(1)}, bf16[256,768]{1,0:T(8,128)(2,1)S(1)}, u32[]{:S(2)}, u32[]{:S(2)}) collective-permute-start(bf16[256,768]{1,0:T(8,128)(2,1)S(1)} %get-tuple-element.266), channel_id=1, source_target_pairs={{0,8},{4,12},{8,16},{12,20},{1,9},{5,13},{9,17},{13,21},{2,10},{6,... | collective-permute-start | bytes 1179656 | tf_op jit(solution)/shard_map/ppermute | solution.py:464
  9.9 2.1 collective-permute-start.2
  18.5 7.2 %collective-permute-start.15 = (bf16[768,768]{1,0:T(8,128)(2,1)}, bf16[768,768]{1,0:T(8,128)(2,1)}, u32[]{:S(2)}, u32[]{:S(2)}) collective-permute-start(bf16[768,768]{1,0:T(8,128)(2,1)} %bitcast.18), channel_id=1, source_target_pairs={{0,16},{16,0},{1,17},{17,1},{2,18},{18,2},{3,19},{19,3},{4,20},{20... | collective-permute-start | bytes 3538952 | tf_op jit(solution)/shard_map/ppermute | solution.py:48
  28.5 2.5 copy.83
  31.0 1.8 bitcast_select_fusion.1
  33.5 1.9 collective-permute-start.4
  36.9 4.1 collective-permute-done.4.refs_5_.refs_10_
  41.0 1.9 broadcast_select_fusion.4
  44.9 1.5 collective-permute-start.20
  46.5 2.2 attend_enc.1
  53.5 2.8 broadcast_select_fusion
  61.2 1.8 collective-permute-start.13
  62.9 2.8 broadcast_select_fusion.1
  66.8 1.7 ffn_enc.1
  77.2 1.7 collective-permute-done.18.refs_3_
  81.6 1.9 norm_end_enc.1
  85.2 1.8 collective-permute-start.31
  87.0 1.6 select_bitcast_fusion.6
  88.8 5.8 %collective-permute-start.44 = (bf16[64,768]{1,0:T(8,128)(2,1)}, bf16[64,768]{1,0:T(8,128)(2,1)}, u32[]{:S(2)}, u32[]{:S(2)}) collective-permute-start(bf16[64,768]{1,0:T(8,128)(2,1)} %select_bitcast_fusion.6), channel_id=1, source_target_pairs={{0,8},{4,12},{24,16},{28,20},{1,9},{5,13},{25,17},{29,21},{2,10},{... | collective-permute-start | bytes 294920 | tf_op jit(solution)/shard_map/ppermute | solution.py:586
  96.6 1.7 copy.119.refs_3_.refs_8_
  103.4 3.6 attend_dec.1
  108.8 1.8 collective-permute-start.25
  111.7 3.0 collective-permute-done.24.refs_2_
  120.8 1.9 collective-permute-done.28.refs_3_
  123.1 3.4 attend_cross.1
  132.0 2.1 collective-permute-done.37.refs_3_
  137.9 1.6 collective-permute-done.38.refs_1_
  140.2 1.7 collective-permute-done.40.refs_3_
  148.4 3.0 collective-permute-done.43.refs_3_
  163.3 2.9 grad_ffn_dec.1
  167.4 2.8 collective-permute-start.99
  170.2 1.6 collective-permute-done.53.refs_3_
  173.8 1.8 collective-permute-start.56
  177.5 1.8 collective-permute-done.56.refs_3_
  179.3 4.2 attend_back_cross.1
  183.6 13.7 %all_gather.6 = bf16[2,256,768]{2,1,0:T(8,128)(2,1)} all-gather(bf16[2,64,768]{2,1,0:T(8,128)(2,1)S(1)} %pad_maximum_fusion.12), channel_id=1, replica_groups=mesh['section'=2,'seq'=4,'tp'=4] {'tp'}, dimensions={1}, use_global_device_ids=true | all-gather | bytes 983040 | tf_op jit(solution)/shard_map/all_gather | solution.py:654
  201.8 2.0 collective-permute-done.76.refs_1_
  210.4 2.0 collective-permute-start.58
  214.4 4.5 attend_back_dec.1
  225.4 2.2 collective-permute-done.60.refs_2_
  233.4 1.9 collective-permute-start.83
  248.5 4.0 concatenate.77
  252.6 40.6 %psum.7 = f32[20,768]{1,0:T(8,128)} all-reduce(f32[20,768]{1,0:T(8,128)} %concatenate.77), channel_id=1, replica_groups=mesh['section'=2,'seq'=4,'tp'=4] {'section','seq','tp'}, use_global_device_ids=true, to_apply=%region_0.1 | all-reduce | flops 15360 | bytes 122880 | tf_op jit(solution)/shard_map/psum | solution.py:726
  295.6 2.3 collective-permute-start.68
  313.1 3.2 attend_back_enc.1
  320.7 7.6 %collective-permute-done.103 = bf16[192,768]{1,0:T(8,128)(2,1)S(1)} collective-permute-done((bf16[192,768]{1,0:T(8,128)(2,1)S(1)}, bf16[192,768]{1,0:T(8,128)(2,1)S(1)}, u32[]{:S(2)}, u32[]{:S(2)}) %collective-permute-start.103) | collective-permute-done | bytes 294944 | tf_op jit(solution)/shard_map/ppermute | solution.py:668
  328.8 6.1 %collective-permute-done.72 = bf16[256,384]{1,0:T(8,128)(2,1)S(1)} collective-permute-done((bf16[256,384]{1,0:T(8,128)(2,1)S(1)}, bf16[256,384]{1,0:T(8,128)(2,1)S(1)}, u32[]{:S(2)}, u32[]{:S(2)}) %collective-permute-start.72) | collective-permute-done | bytes 196640 | tf_op jit(solution)/shard_map/ppermute | solution.py:52
  341.4 1.9 collective-permute-done.104
  344.5 4.1 collective-permute-start.93
  349.7 1.9 collective-permute-start.87
  352.4 1.6 copy.95
  356.0 1.7 pad_maximum_fusion.11
  357.8 5.0 %collective-permute-done.88 = bf16[64,768]{1,0:T(8,128)(2,1)S(1)} collective-permute-done((bf16[64,768]{1,0:T(8,128)(2,1)}, bf16[64,768]{1,0:T(8,128)(2,1)S(1)}, u32[]{:S(2)}, u32[]{:S(2)}) %collective-permute-start.88) | collective-permute-done | bytes 98336 | tf_op jit(solution)/shard_map/ppermute | solution.py:472
  365.0 13.8 %all_gather.7 = bf16[2,256,768]{2,1,0:T(8,128)(2,1)} all-gather(bf16[2,64,768]{2,1,0:T(8,128)(2,1)S(1)} %pad_maximum_fusion.13), channel_id=1, replica_groups=mesh['section'=2,'seq'=4,'tp'=4] {'tp'}, dimensions={1}, use_global_device_ids=true | all-gather | bytes 983040 | tf_op jit(solution)/shard_map/all_gather | solution.py:654
  378.8 1.6 add_convert_fusion.4
  381.1 3.0 add_convert_fusion
  385.0 2.3 add_convert_fusion.1
  387.4 2.1 collective-permute-start.97
  389.8 3.9 collective-permute-start.91
  397.2 30.0 %collective-permute-done.91 = bf16[384,768]{1,0:T(8,128)(2,1)S(1)} collective-permute-done((bf16[384,768]{1,0:T(8,128)(2,1)S(1)}, bf16[384,768]{1,0:T(8,128)(2,1)S(1)}, u32[]{:S(2)}, u32[]{:S(2)}) %collective-permute-start.91) | collective-permute-done | bytes 589856 | tf_op jit(solution)/shard_map/ppermute | solution.py:668
  427.4 3.7 collective-permute-start.92
  432.3 3.0 collective-permute-start.98
  435.3 13.4 %collective-permute-done.92 = bf16[192,768]{1,0:T(8,128)(2,1)S(1)} collective-permute-done((bf16[192,768]{1,0:T(8,128)(2,1)S(1)}, bf16[192,768]{1,0:T(8,128)(2,1)S(1)}, u32[]{:S(2)}, u32[]{:S(2)}) %collective-permute-start.92) | collective-permute-done | bytes 294944 | tf_op jit(solution)/shard_map/ppermute | solution.py:668
  450.7 4.4 collective-permute-done.98
  (564 shorter events, 177.8 us)
Async XLA Ops:
  1.9 16.6 %collective-permute-start.1 = (bf16[256,768]{1,0:T(8,128)(2,1)S(1)}, bf16[256,768]{1,0:T(8,128)(2,1)S(1)}, u32[]{:S(2)}, u32[]{:S(2)}) collective-permute-start(bf16[256,768]{1,0:T(8,128)(2,1)S(1)} %get-tuple-element.266), channel_id=1, source_target_pairs={{0,8},{4,12},{8,16},{12,20},{1,9},{5,13},{9,17},{13,21},{2,10},{6,... | collective-permute-start | bytes 1179656 | tf_op jit(solution)/shard_map/ppermute | solution.py:464
  7.9 17.8 %collective-permute-start.19 = (bf16[256,768]{1,0:T(8,128)(2,1)S(1)}, bf16[256,768]{1,0:T(8,128)(2,1)S(1)}, u32[]{:S(2)}, u32[]{:S(2)}) collective-permute-start(bf16[256,768]{1,0:T(8,128)(2,1)S(1)} %get-tuple-element.266), channel_id=1, source_target_pairs={{16,8},{20,12},{24,16},{28,20},{17,9},{21,13},{25,17},{29,21},{18,... | collective-permute-start | bytes 1179656 | tf_op jit(solution)/shard_map/ppermute | solution.py:466
  8.6 9.4 %collective-permute-start = (bf16[256,768]{1,0:T(8,128)(2,1)S(1)}, bf16[256,768]{1,0:T(8,128)(2,1)}, u32[]{:S(2)}, u32[]{:S(2)}) collective-permute-start(bf16[256,768]{1,0:T(8,128)(2,1)S(1)} %get-tuple-element.265), channel_id=1, source_target_pairs={{8,24},{12,28},{16,0},{20,4},{9,25},{13,29},{17,1},{21,5},{10,26},... | collective-permute-start | bytes 1179656 | tf_op jit(solution)/shard_map/ppermute | solution.py:465
  9.9 18.6 %collective-permute-start.2 = (bf16[3,768,192]{1,2,0:T(8,128)(2,1)S(1)}, bf16[3,768,192]{1,2,0:T(8,128)(2,1)}, u32[]{:S(2)}, u32[]{:S(2)}) collective-permute-start(bf16[3,768,192]{1,2,0:T(8,128)(2,1)S(1)} %bitcast.186), channel_id=1, source_target_pairs={{0,16},{16,0},{1,17},{17,1},{2,18},{18,2},{3,19},{19,3},{4,20},{20... | collective-permute-start | bytes 2654216 | tf_op jit(solution)/shard_map/ppermute | solution.py:48
  12.0 29.0 %collective-permute-start.3 = (bf16[192,768]{1,0:T(8,128)(2,1)}, bf16[192,768]{1,0:T(8,128)(2,1)}, u32[]{:S(2)}, u32[]{:S(2)}) collective-permute-start(bf16[192,768]{1,0:T(8,128)(2,1)} %bitcast.9), channel_id=1, source_target_pairs={{0,16},{16,0},{1,17},{17,1},{2,18},{18,2},{3,19},{19,3},{4,20},{20... | collective-permute-start | bytes 884744 | tf_op jit(solution)/shard_map/ppermute | solution.py:48
  18.0 17.4 %collective-permute-start.10 = (f32[8,768]{1,0:T(8,128)}, f32[8,768]{1,0:T(8,128)}, u32[]{:S(2)}, u32[]{:S(2)}) collective-permute-start(f32[8,768]{1,0:T(8,128)} %maximum_maximum_fusion), channel_id=1, source_target_pairs={{0,16},{16,0},{1,17},{17,1},{2,18},{18,2},{3,19},{19,3},{4,20},{20... | collective-permute-start | bytes 73736 | tf_op jit(solution)/shard_map/ppermute | solution.py:48
  18.5 34.5 %collective-permute-start.15 = (bf16[768,768]{1,0:T(8,128)(2,1)}, bf16[768,768]{1,0:T(8,128)(2,1)}, u32[]{:S(2)}, u32[]{:S(2)}) collective-permute-start(bf16[768,768]{1,0:T(8,128)(2,1)} %bitcast.18), channel_id=1, source_target_pairs={{0,16},{16,0},{1,17},{17,1},{2,18},{18,2},{3,19},{19,3},{4,20},{20... | collective-permute-start | bytes 3538952 | tf_op jit(solution)/shard_map/ppermute | solution.py:48
  26.5 36.5 %collective-permute-start.14 = (bf16[768,768]{1,0:T(8,128)(2,1)}, bf16[768,768]{1,0:T(8,128)(2,1)}, u32[]{:S(2)}, u32[]{:S(2)}) collective-permute-start(bf16[768,768]{1,0:T(8,128)(2,1)} %bitcast.17), channel_id=1, source_target_pairs={{0,16},{16,0},{1,17},{17,1},{2,18},{18,2},{3,19},{19,3},{4,20},{20... | collective-permute-start | bytes 3538952 | tf_op jit(solution)/shard_map/ppermute | solution.py:48
  33.5 7.5 %collective-permute-start.4 = (bf16[256,384]{1,0:T(8,128)(2,1)S(1)}, bf16[256,384]{1,0:T(8,128)(2,1)S(1)}, u32[]{:S(2)}, u32[]{:S(2)}) collective-permute-start(bf16[256,384]{1,0:T(8,128)(2,1)S(1)} %get-tuple-element.112.refs_4_.refs_9_), channel_id=1, source_target_pairs={{0,4},{4,0},{8,12},{12,8},{1,5},{5,1},{9,13},{13,9},{2,6},{6,2},{1... | collective-permute-start | bytes 589832 | tf_op jit(solution)/shard_map/ppermute | solution.py:52
  36.8 9.6 %collective-permute-start.5 = (bf16[256,384]{1,0:T(8,128)(2,1)S(1)}, bf16[256,384]{1,0:T(8,128)(2,1)S(1)}, u32[]{:S(2)}, u32[]{:S(2)}) collective-permute-start(bf16[256,384]{1,0:T(8,128)(2,1)S(1)} %get-tuple-element.112.refs_4_.refs_9_), channel_id=1, source_target_pairs={{0,16},{16,0},{1,17},{17,1},{2,18},{18,2},{3,19},{19,3},{4,20},{20... | collective-permute-start | bytes 589832 | tf_op jit(solution)/shard_map/ppermute | solution.py:48
  44.9 31.7 %collective-permute-start.20 = (bf16[256,384]{1,0:T(8,128)(2,1)}, bf16[256,384]{1,0:T(8,128)(2,1)}, u32[]{:S(2)}, u32[]{:S(2)}) collective-permute-start(bf16[256,384]{1,0:T(8,128)(2,1)} %get-tuple-element.125.refs_6_.refs_11_), channel_id=1, source_target_pairs={{0,4},{4,0},{8,12},{12,8},{1,5},{5,1},{9,13},{13,9},{2,6},{6,2},{1... | collective-permute-start | bytes 589832 | tf_op jit(solution)/shard_map/ppermute | solution.py:52
  50.0 6.3 %collective-permute-start.7 = (bf16[64,768]{1,0:T(8,128)(2,1)S(1)}, bf16[64,768]{1,0:T(8,128)(2,1)S(1)}, u32[]{:S(2)}, u32[]{:S(2)}) collective-permute-start(bf16[64,768]{1,0:T(8,128)(2,1)S(1)} %get-tuple-element.114), channel_id=1, source_target_pairs={{0,1},{1,0},{2,3},{3,2},{4,5},{5,4},{6,7},{7,6},{8,9},{9,8},{10,11... | collective-permute-start | bytes 294920 | tf_op jit(solution)/shard_map/ppermute | solution.py:52
  59.5 6.3 %collective-permute-start.11 = (bf16[64,768]{1,0:T(8,128)(2,1)S(1)}, bf16[64,768]{1,0:T(8,128)(2,1)S(1)}, u32[]{:S(2)}, u32[]{:S(2)}) collective-permute-start(bf16[64,768]{1,0:T(8,128)(2,1)S(1)} %get-tuple-element.117.refs_0_), channel_id=1, source_target_pairs={{0,1},{1,0},{2,3},{3,2},{4,5},{5,4},{6,7},{7,6},{8,9},{9,8},{10,11... | collective-permute-start | bytes 294920 | tf_op jit(solution)/shard_map/ppermute | solution.py:52
  70.8 6.3 %collective-permute-start.16 = (bf16[64,768]{1,0:T(8,128)(2,1)}, bf16[64,768]{1,0:T(8,128)(2,1)}, u32[]{:S(2)}, u32[]{:S(2)}) collective-permute-start(bf16[64,768]{1,0:T(8,128)(2,1)} %get-tuple-element.119), channel_id=1, source_target_pairs={{0,1},{1,0},{2,3},{3,2},{4,5},{5,4},{6,7},{7,6},{8,9},{9,8},{10,11... | collective-permute-start | bytes 294920 | tf_op jit(solution)/shard_map/ppermute | solution.py:52
  73.1 5.8 %collective-permute-start.18 = (bf16[64,768]{1,0:T(8,128)(2,1)}, bf16[64,768]{1,0:T(8,128)(2,1)}, u32[]{:S(2)}, u32[]{:S(2)}) collective-permute-start(bf16[64,768]{1,0:T(8,128)(2,1)} %get-tuple-element.121), channel_id=1, source_target_pairs={{0,3},{1,2},{2,1},{3,0},{4,7},{5,6},{6,5},{7,4},{8,11},{9,10},{10,... | collective-permute-start | bytes 294920 | tf_op jit(solution)/shard_map/ppermute | solution.py:52
  76.5 22.9 %collective-permute-start.21 = (bf16[256,384]{1,0:T(8,128)(2,1)}, bf16[256,384]{1,0:T(8,128)(2,1)}, u32[]{:S(2)}, u32[]{:S(2)}) collective-permute-start(bf16[256,384]{1,0:T(8,128)(2,1)} %get-tuple-element.125.refs_6_.refs_11_), channel_id=1, source_target_pairs={{0,16},{16,0},{1,17},{17,1},{2,18},{18,2},{3,19},{19,3},{4,20},{20... | collective-permute-start | bytes 589832 | tf_op jit(solution)/shard_map/ppermute | solution.py:48
  76.6 22.9 %collective-permute-start.22 = (bf16[256,384]{1,0:T(8,128)(2,1)}, bf16[256,384]{1,0:T(8,128)(2,1)}, u32[]{:S(2)}, u32[]{:S(2)}) collective-permute-start(bf16[256,384]{1,0:T(8,128)(2,1)} %collective-permute-done.20.refs_7_.refs_12_), channel_id=1, source_target_pairs={{0,16},{16,0},{1,17},{17,1},{2,18},{18,2},{3,19},{19,3},{4,20},{20... | collective-permute-start | bytes 589832 | tf_op jit(solution)/shard_map/ppermute | solution.py:48
  84.3 10.3 %collective-permute-start.30 = (bf16[64,768]{1,0:T(8,128)(2,1)S(1)}, bf16[64,768]{1,0:T(8,128)(2,1)S(1)}, u32[]{:S(2)}, u32[]{:S(2)}) collective-permute-start(bf16[64,768]{1,0:T(8,128)(2,1)S(1)} %get-tuple-element.123.refs_0_), channel_id=1, source_target_pairs={{0,2},{1,3},{2,0},{3,1},{4,6},{5,7},{6,4},{7,5},{8,10},{9,11},{10,... | collective-permute-start | bytes 294920 | tf_op jit(solution)/shard_map/ppermute | solution.py:52
  85.2 9.4 %collective-permute-start.31 = (bf16[64,768]{1,0:T(8,128)(2,1)S(1)}, bf16[64,768]{1,0:T(8,128)(2,1)S(1)}, u32[]{:S(2)}, u32[]{:S(2)}) collective-permute-start(bf16[64,768]{1,0:T(8,128)(2,1)S(1)} %get-tuple-element.123.refs_0_), channel_id=1, source_target_pairs={{0,3},{1,2},{2,1},{3,0},{4,7},{5,6},{6,5},{7,4},{8,11},{9,10},{10,... | collective-permute-start | bytes 294920 | tf_op jit(solution)/shard_map/ppermute | solution.py:52
  88.8 29.8 %collective-permute-start.44 = (bf16[64,768]{1,0:T(8,128)(2,1)}, bf16[64,768]{1,0:T(8,128)(2,1)}, u32[]{:S(2)}, u32[]{:S(2)}) collective-permute-start(bf16[64,768]{1,0:T(8,128)(2,1)} %select_bitcast_fusion.6), channel_id=1, source_target_pairs={{0,8},{4,12},{24,16},{28,20},{1,9},{5,13},{25,17},{29,21},{2,10},{... | collective-permute-start | bytes 294920 | tf_op jit(solution)/shard_map/ppermute | solution.py:586
  95.8 22.8 %collective-permute-start.32 = (bf16[256,384]{1,0:T(8,128)(2,1)}, bf16[256,384]{1,0:T(8,128)(2,1)}, u32[]{:S(2)}, u32[]{:S(2)}) collective-permute-start(bf16[256,384]{1,0:T(8,128)(2,1)} %kv_cross.1.refs_4_.refs_9_), channel_id=1, source_target_pairs={{0,4},{4,0},{8,12},{12,8},{1,5},{5,1},{9,13},{13,9},{2,6},{6,2},{1... | collective-permute-start | bytes 589832 | tf_op jit(solution)/shard_map/ppermute | solution.py:52
  107.8 7.0 %collective-permute-start.24 = (bf16[64,768]{1,0:T(8,128)(2,1)S(1)}, bf16[64,768]{1,0:T(8,128)(2,1)S(1)}, u32[]{:S(2)}, u32[]{:S(2)}) collective-permute-start(bf16[64,768]{1,0:T(8,128)(2,1)S(1)} %get-tuple-element.128), channel_id=1, source_target_pairs={{0,2},{1,3},{2,0},{3,1},{4,6},{5,7},{6,4},{7,5},{8,10},{9,11},{10,... | collective-permute-start | bytes 294920 | tf_op jit(solution)/shard_map/ppermute | solution.py:52
  108.8 5.9 %collective-permute-start.25 = (bf16[64,768]{1,0:T(8,128)(2,1)S(1)}, bf16[64,768]{1,0:T(8,128)(2,1)S(1)}, u32[]{:S(2)}, u32[]{:S(2)}) collective-permute-start(bf16[64,768]{1,0:T(8,128)(2,1)S(1)} %get-tuple-element.129), channel_id=1, source_target_pairs={{0,3},{1,2},{2,1},{3,0},{4,7},{5,6},{6,5},{7,4},{8,11},{9,10},{10,... | collective-permute-start | bytes 294920 | tf_op jit(solution)/shard_map/ppermute | solution.py:52
  130.1 36.1 %collective-permute-start.46 = (bf16[64,768]{1,0:T(8,128)(2,1)S(1)}, bf16[64,768]{1,0:T(8,128)(2,1)S(1)}, u32[]{:S(2)}, u32[]{:S(2)}) collective-permute-start(bf16[64,768]{1,0:T(8,128)(2,1)S(1)} %copy-done.15), channel_id=1, source_target_pairs={{8,0},{12,4},{16,8},{20,12},{9,1},{13,5},{17,9},{21,13},{10,2},{14... | collective-permute-start | bytes 294920 | tf_op jit(solution)/shard_map/ppermute | solution.py:472
  145.0 6.4 %collective-permute-start.43 = (bf16[64,768]{1,0:T(8,128)(2,1)S(1)}, bf16[64,768]{1,0:T(8,128)(2,1)S(1)}, u32[]{:S(2)}, u32[]{:S(2)}) collective-permute-start(bf16[64,768]{1,0:T(8,128)(2,1)S(1)} %get-tuple-element.140), channel_id=1, source_target_pairs={{0,3},{1,2},{2,1},{3,0},{4,7},{5,6},{6,5},{7,4},{8,11},{9,10},{10,... | collective-permute-start | bytes 294920 | tf_op jit(solution)/shard_map/ppermute | solution.py:52
  156.5 13.6 %collective-permute-start.47 = (bf16[64,768]{1,0:T(8,128)(2,1)S(1)}, bf16[64,768]{1,0:T(8,128)(2,1)S(1)}, u32[]{:S(2)}, u32[]{:S(2)}) collective-permute-start(bf16[64,768]{1,0:T(8,128)(2,1)S(1)} %get-tuple-element.142), channel_id=1, source_target_pairs={{8,16},{12,20},{16,24},{20,28},{9,17},{13,21},{17,25},{21,29},{10,... | collective-permute-start | bytes 294920 | tf_op jit(solution)/shard_map/ppermute | solution.py:473
  157.2 10.1 %collective-permute-start.45 = (bf16[64,768]{1,0:T(8,128)(2,1)S(1)}, bf16[64,768]{1,0:T(8,128)(2,1)S(1)}, u32[]{:S(2)}, u32[]{:S(2)}) collective-permute-start(bf16[64,768]{1,0:T(8,128)(2,1)S(1)} %broadcast_select_fusion.9), channel_id=1, source_target_pairs={{24,8},{28,12},{0,16},{4,20},{25,9},{29,13},{1,17},{5,21},{26,10},... | collective-permute-start | bytes 294920 | tf_op jit(solution)/shard_map/ppermute | solution.py:474
  160.9 9.3 %collective-permute-start.51 = (bf16[64,768]{1,0:T(8,128)(2,1)S(1)}, bf16[64,768]{1,0:T(8,128)(2,1)S(1)}, u32[]{:S(2)}, u32[]{:S(2)}) collective-permute-start(bf16[64,768]{1,0:T(8,128)(2,1)S(1)} %get-tuple-element.146), channel_id=1, source_target_pairs={{0,1},{1,0},{2,3},{3,2},{4,5},{5,4},{6,7},{7,6},{8,9},{9,8},{10,11... | collective-permute-start | bytes 294920 | tf_op jit(solution)/shard_map/ppermute | solution.py:52
  162.2 8.0 %collective-permute-start.52 = (bf16[64,768]{1,0:T(8,128)(2,1)S(1)}, bf16[64,768]{1,0:T(8,128)(2,1)S(1)}, u32[]{:S(2)}, u32[]{:S(2)}) collective-permute-start(bf16[64,768]{1,0:T(8,128)(2,1)S(1)} %get-tuple-element.147), channel_id=1, source_target_pairs={{0,2},{1,3},{2,0},{3,1},{4,6},{5,7},{6,4},{7,5},{8,10},{9,11},{10,... | collective-permute-start | bytes 294920 | tf_op jit(solution)/shard_map/ppermute | solution.py:52
  167.4 213.8 %collective-permute-start.99 = (bf16[768,1536]{1,0:T(8,128)(2,1)}, bf16[768,1536]{1,0:T(8,128)(2,1)}, u32[]{:S(2)}, u32[]{:S(2)}) collective-permute-start(bf16[768,1536]{1,0:T(8,128)(2,1)} %grad_ffn_dec.1), channel_id=1, source_target_pairs={{0,16},{1,17},{2,18},{3,19},{4,20},{5,21},{6,22},{7,23},{8,24},{9,... | collective-permute-start | bytes 7077896 | tf_op jit(solution)/shard_map/ppermute | solution.py:677
  183.5 26.8 %collective-permute-start.57 = (bf16[512,384]{1,0:T(8,128)(2,1)S(1)}, bf16[512,384]{1,0:T(8,128)(2,1)S(1)}, u32[]{:S(2)}, u32[]{:S(2)}) collective-permute-start(bf16[512,384]{1,0:T(8,128)(2,1)S(1)} %get-tuple-element.154), channel_id=1, source_target_pairs={{0,16},{16,0},{1,17},{17,1},{2,18},{18,2},{3,19},{19,3},{4,20},{20... | collective-permute-start | bytes 1179656 | tf_op jit(solution)/shard_map/ppermute | solution.py:48
  206.8 6.2 %collective-permute-start.79 = (bf16[64,768]{1,0:T(8,128)(2,1)S(1)}, bf16[64,768]{1,0:T(8,128)(2,1)S(1)}, u32[]{:S(2)}, u32[]{:S(2)}) collective-permute-start(bf16[64,768]{1,0:T(8,128)(2,1)S(1)} %get-tuple-element.185.refs_0_), channel_id=1, source_target_pairs={{0,1},{1,0},{2,3},{3,2},{4,5},{5,4},{6,7},{7,6},{8,9},{9,8},{10,11... | collective-permute-start | bytes 294920 | tf_op jit(solution)/shard_map/ppermute | solution.py:52
  210.4 8.5 %collective-permute-start.58 = (bf16[256,384]{1,0:T(8,128)(2,1)S(1)}, bf16[256,384]{1,0:T(8,128)(2,1)S(1)}, u32[]{:S(2)}, u32[]{:S(2)}) collective-permute-start(bf16[256,384]{1,0:T(8,128)(2,1)S(1)} %slice.378), channel_id=1, source_target_pairs={{0,4},{4,0},{8,12},{12,8},{1,5},{5,1},{9,13},{13,9},{2,6},{6,2},{1... | collective-permute-start | bytes 589832 | tf_op jit(solution)/shard_map/ppermute | solution.py:52
  218.9 11.1 %collective-permute-start.82 = (bf16[512,384]{1,0:T(8,128)(2,1)S(1)}, bf16[512,384]{1,0:T(8,128)(2,1)S(1)}, u32[]{:S(2)}, u32[]{:S(2)}) collective-permute-start(bf16[512,384]{1,0:T(8,128)(2,1)S(1)} %get-tuple-element.189), channel_id=1, source_target_pairs={{0,16},{16,0},{1,17},{17,1},{2,18},{18,2},{3,19},{19,3},{4,20},{20... | collective-permute-start | bytes 1179656 | tf_op jit(solution)/shard_map/ppermute | solution.py:48
  219.4 6.0 %collective-permute-start.59 = (bf16[64,768]{1,0:T(8,128)(2,1)S(1)}, bf16[64,768]{1,0:T(8,128)(2,1)S(1)}, u32[]{:S(2)}, u32[]{:S(2)}) collective-permute-start(bf16[64,768]{1,0:T(8,128)(2,1)S(1)} %get-tuple-element.156), channel_id=1, source_target_pairs={{0,1},{1,0},{2,3},{3,2},{4,5},{5,4},{6,7},{7,6},{8,9},{9,8},{10,11... | collective-permute-start | bytes 294920 | tf_op jit(solution)/shard_map/ppermute | solution.py:52
  220.5 7.0 %collective-permute-start.60 = (bf16[64,768]{1,0:T(8,128)(2,1)S(1)}, bf16[64,768]{1,0:T(8,128)(2,1)S(1)}, u32[]{:S(2)}, u32[]{:S(2)}) collective-permute-start(bf16[64,768]{1,0:T(8,128)(2,1)S(1)} %get-tuple-element.157), channel_id=1, source_target_pairs={{0,2},{1,3},{2,0},{3,1},{4,6},{5,7},{6,4},{7,5},{8,10},{9,11},{10,... | collective-permute-start | bytes 294920 | tf_op jit(solution)/shard_map/ppermute | solution.py:52
  221.5 6.0 %collective-permute-start.61 = (bf16[64,768]{1,0:T(8,128)(2,1)S(1)}, bf16[64,768]{1,0:T(8,128)(2,1)S(1)}, u32[]{:S(2)}, u32[]{:S(2)}) collective-permute-start(bf16[64,768]{1,0:T(8,128)(2,1)S(1)} %get-tuple-element.158), channel_id=1, source_target_pairs={{0,3},{1,2},{2,1},{3,0},{4,7},{5,6},{6,5},{7,4},{8,11},{9,10},{10,... | collective-permute-start | bytes 294920 | tf_op jit(solution)/shard_map/ppermute | solution.py:52
  225.4 92.2 %collective-permute-start.102 = (bf16[384,768]{1,0:T(8,128)(2,1)}, bf16[384,768]{1,0:T(8,128)(2,1)}, u32[]{:S(2)}, u32[]{:S(2)}) collective-permute-start(bf16[384,768]{1,0:T(8,128)(2,1)} %slice.324), channel_id=1, source_target_pairs={{0,16},{16,0},{1,17},{17,1},{2,18},{18,2},{3,19},{19,3},{4,20},{20... | collective-permute-start | bytes 1769480 | tf_op jit(solution)/shard_map/ppermute | solution.py:48
  228.9 6.5 %collective-permute-start.63 = (bf16[64,768]{1,0:T(8,128)(2,1)S(1)}, bf16[64,768]{1,0:T(8,128)(2,1)S(1)}, u32[]{:S(2)}, u32[]{:S(2)}) collective-permute-start(bf16[64,768]{1,0:T(8,128)(2,1)S(1)} %get-tuple-element.160.refs_0_), channel_id=1, source_target_pairs={{0,2},{1,3},{2,0},{3,1},{4,6},{5,7},{6,4},{7,5},{8,10},{9,11},{10,... | collective-permute-start | bytes 294920 | tf_op jit(solution)/shard_map/ppermute | solution.py:52
  233.4 6.0 %collective-permute-start.83 = (bf16[256,384]{1,0:T(8,128)(2,1)S(1)}, bf16[256,384]{1,0:T(8,128)(2,1)S(1)}, u32[]{:S(2)}, u32[]{:S(2)}) collective-permute-start(bf16[256,384]{1,0:T(8,128)(2,1)S(1)} %slice.376), channel_id=1, source_target_pairs={{0,4},{4,0},{8,12},{12,8},{1,5},{5,1},{9,13},{13,9},{2,6},{6,2},{1... | collective-permute-start | bytes 589832 | tf_op jit(solution)/shard_map/ppermute | solution.py:52
  236.7 9.6 %collective-permute-start.65 = (bf16[64,768]{1,0:T(8,128)(2,1)S(1)}, bf16[64,768]{1,0:T(8,128)(2,1)S(1)}, u32[]{:S(2)}, u32[]{:S(2)}) collective-permute-start(bf16[64,768]{1,0:T(8,128)(2,1)S(1)} %get-tuple-element.163), channel_id=1, source_target_pairs={{0,1},{1,0},{2,3},{3,2},{4,5},{5,4},{6,7},{7,6},{8,9},{9,8},{10,11... | collective-permute-start | bytes 294920 | tf_op jit(solution)/shard_map/ppermute | solution.py:52
  237.7 8.6 %collective-permute-start.66 = (bf16[64,768]{1,0:T(8,128)(2,1)S(1)}, bf16[64,768]{1,0:T(8,128)(2,1)S(1)}, u32[]{:S(2)}, u32[]{:S(2)}) collective-permute-start(bf16[64,768]{1,0:T(8,128)(2,1)S(1)} %get-tuple-element.164), channel_id=1, source_target_pairs={{0,2},{1,3},{2,0},{3,1},{4,6},{5,7},{6,4},{7,5},{8,10},{9,11},{10,... | collective-permute-start | bytes 294920 | tf_op jit(solution)/shard_map/ppermute | solution.py:52
  239.4 6.8 %collective-permute-start.67 = (bf16[64,768]{1,0:T(8,128)(2,1)S(1)}, bf16[64,768]{1,0:T(8,128)(2,1)S(1)}, u32[]{:S(2)}, u32[]{:S(2)}) collective-permute-start(bf16[64,768]{1,0:T(8,128)(2,1)S(1)} %get-tuple-element.165), channel_id=1, source_target_pairs={{0,3},{1,2},{2,1},{3,0},{4,7},{5,6},{6,5},{7,4},{8,11},{9,10},{10,... | collective-permute-start | bytes 294920 | tf_op jit(solution)/shard_map/ppermute | solution.py:52
  298.9 6.0 %collective-permute-start.70 = (bf16[64,768]{1,0:T(8,128)(2,1)}, bf16[64,768]{1,0:T(8,128)(2,1)S(1)}, u32[]{:S(2)}, u32[]{:S(2)}) collective-permute-start(bf16[64,768]{1,0:T(8,128)(2,1)} %copy-done.68), channel_id=1, source_target_pairs={{0,3},{1,2},{2,1},{3,0},{4,7},{5,6},{6,5},{7,4},{8,11},{9,10},{10,... | collective-permute-start | bytes 294920 | tf_op jit(solution)/shard_map/ppermute | solution.py:52
  301.2 36.8 %collective-permute-start.84 = (bf16[64,768]{1,0:T(8,128)(2,1)}, bf16[64,768]{1,0:T(8,128)(2,1)S(1)}, u32[]{:S(2)}, u32[]{:S(2)}) collective-permute-start(bf16[64,768]{1,0:T(8,128)(2,1)} %copy-done.89), channel_id=1, source_target_pairs={{0,1},{1,0},{2,3},{3,2},{4,5},{5,4},{6,7},{7,6},{8,9},{9,8},{10,11... | collective-permute-start | bytes 294920 | tf_op jit(solution)/shard_map/ppermute | solution.py:52
  303.1 36.5 %collective-permute-start.85 = (bf16[64,768]{1,0:T(8,128)(2,1)}, bf16[64,768]{1,0:T(8,128)(2,1)S(1)}, u32[]{:S(2)}, u32[]{:S(2)}) collective-permute-start(bf16[64,768]{1,0:T(8,128)(2,1)} %copy-done.88), channel_id=1, source_target_pairs={{0,2},{1,3},{2,0},{3,1},{4,6},{5,7},{6,4},{7,5},{8,10},{9,11},{10,... | collective-permute-start | bytes 294920 | tf_op jit(solution)/shard_map/ppermute | solution.py:52
  318.9 9.5 %collective-permute-start.103 = (bf16[192,768]{1,0:T(8,128)(2,1)S(1)}, bf16[192,768]{1,0:T(8,128)(2,1)S(1)}, u32[]{:S(2)}, u32[]{:S(2)}) collective-permute-start(bf16[192,768]{1,0:T(8,128)(2,1)S(1)} %slice.326), channel_id=1, source_target_pairs={{0,4},{4,0},{8,12},{12,8},{16,20},{20,16},{24,28},{28,24},{1,5},{5... | collective-permute-start | bytes 884744 | tf_op jit(solution)/shard_map/ppermute | solution.py:668
  319.3 21.3 %collective-permute-start.86 = (bf16[64,768]{1,0:T(8,128)(2,1)S(1)}, bf16[64,768]{1,0:T(8,128)(2,1)S(1)}, u32[]{:S(2)}, u32[]{:S(2)}) collective-permute-start(bf16[64,768]{1,0:T(8,128)(2,1)S(1)} %copy-done.87), channel_id=1, source_target_pairs={{0,3},{1,2},{2,1},{3,0},{4,7},{5,6},{6,5},{7,4},{8,11},{9,10},{10,... | collective-permute-start | bytes 294920 | tf_op jit(solution)/shard_map/ppermute | solution.py:52
  328.3 6.5 %collective-permute-start.72 = (bf16[256,384]{1,0:T(8,128)(2,1)S(1)}, bf16[256,384]{1,0:T(8,128)(2,1)S(1)}, u32[]{:S(2)}, u32[]{:S(2)}) collective-permute-start(bf16[256,384]{1,0:T(8,128)(2,1)S(1)} %slice.377), channel_id=1, source_target_pairs={{0,4},{4,0},{8,12},{12,8},{1,5},{5,1},{9,13},{13,9},{2,6},{6,2},{1... | collective-permute-start | bytes 589832 | tf_op jit(solution)/shard_map/ppermute | solution.py:52
  334.9 8.4 %collective-permute-start.104 = (bf16[96,768]{1,0:T(8,128)(2,1)S(1)}, bf16[96,768]{1,0:T(8,128)(2,1)S(1)}, u32[]{:S(2)}, u32[]{:S(2)}) collective-permute-start(bf16[96,768]{1,0:T(8,128)(2,1)S(1)} %slice.328), channel_id=1, source_target_pairs={{0,8},{4,12},{8,0},{12,4},{16,24},{20,28},{24,16},{28,20},{1,9},{5... | collective-permute-start | bytes 442376 | tf_op jit(solution)/shard_map/ppermute | solution.py:668
  338.3 46.7 %collective-permute-start.96 = (bf16[768,1536]{1,0:T(8,128)(2,1)S(1)}, bf16[768,1536]{1,0:T(8,128)(2,1)}, u32[]{:S(2)}, u32[]{:S(2)}) collective-permute-start(bf16[768,1536]{1,0:T(8,128)(2,1)S(1)} %copy-done.7), channel_id=1, source_target_pairs={{16,0},{17,1},{18,2},{19,3},{20,4},{21,5},{22,6},{23,7},{24,8},{25... | collective-permute-start | bytes 7077896 | tf_op jit(solution)/shard_map/ppermute | solution.py:677
  340.6 8.0 %collective-permute-start.74 = (bf16[64,768]{1,0:T(8,128)(2,1)S(1)}, bf16[64,768]{1,0:T(8,128)(2,1)S(1)}, u32[]{:S(2)}, u32[]{:S(2)}) collective-permute-start(bf16[64,768]{1,0:T(8,128)(2,1)S(1)} %get-tuple-element.176), channel_id=1, source_target_pairs={{0,2},{1,3},{2,0},{3,1},{4,6},{5,7},{6,4},{7,5},{8,10},{9,11},{10,... | collective-permute-start | bytes 294920 | tf_op jit(solution)/shard_map/ppermute | solution.py:52
  344.5 34.3 %collective-permute-start.93 = (bf16[768,768]{1,0:T(8,128)(2,1)S(1)}, bf16[768,768]{1,0:T(8,128)(2,1)}, u32[]{:S(2)}, u32[]{:S(2)}) collective-permute-start(bf16[768,768]{1,0:T(8,128)(2,1)S(1)} %grad_self_dec.1), channel_id=1, source_target_pairs={{0,16},{1,17},{2,18},{3,19},{4,20},{5,21},{6,22},{7,23},{8,24},{9,... | collective-permute-start | bytes 3538952 | tf_op jit(solution)/shard_map/ppermute | solution.py:677
  354.1 8.7 %collective-permute-start.88 = (bf16[64,768]{1,0:T(8,128)(2,1)}, bf16[64,768]{1,0:T(8,128)(2,1)S(1)}, u32[]{:S(2)}, u32[]{:S(2)}) collective-permute-start(bf16[64,768]{1,0:T(8,128)(2,1)} %get-tuple-element.251), channel_id=1, source_target_pairs={{8,0},{12,4},{16,8},{20,12},{9,1},{13,5},{17,9},{21,13},{10,2},{14... | collective-permute-start | bytes 294920 | tf_op jit(solution)/shard_map/ppermute | solution.py:472
  355.4 8.7 %collective-permute-start.89 = (bf16[64,768]{1,0:T(8,128)(2,1)}, bf16[64,768]{1,0:T(8,128)(2,1)S(1)}, u32[]{:S(2)}, u32[]{:S(2)}) collective-permute-start(bf16[64,768]{1,0:T(8,128)(2,1)} %get-tuple-element.252), channel_id=1, source_target_pairs={{8,16},{12,20},{16,24},{20,28},{9,17},{13,21},{17,25},{21,29},{10,... | collective-permute-start | bytes 294920 | tf_op jit(solution)/shard_map/ppermute | solution.py:473
  362.7 26.7 %collective-permute-start.90 = (bf16[768,768]{1,0:T(8,128)(2,1)}, bf16[768,768]{1,0:T(8,128)(2,1)S(1)}, u32[]{:S(2)}, u32[]{:S(2)}) collective-permute-start(bf16[768,768]{1,0:T(8,128)(2,1)} %copy-done.12), channel_id=1, source_target_pairs={{16,0},{17,1},{18,2},{19,3},{20,4},{21,5},{22,6},{23,7},{24,8},{25... | collective-permute-start | bytes 3538952 | tf_op jit(solution)/shard_map/ppermute | solution.py:677
  380.4 13.3 %collective-permute-start.94 = (bf16[384,768]{1,0:T(8,128)(2,1)S(1)}, bf16[384,768]{1,0:T(8,128)(2,1)S(1)}, u32[]{:S(2)}, u32[]{:S(2)}) collective-permute-start(bf16[384,768]{1,0:T(8,128)(2,1)S(1)} %slice.300), channel_id=1, source_target_pairs={{16,20},{20,16},{24,28},{28,24},{17,21},{21,17},{25,29},{29,25},{1... | collective-permute-start | bytes 1769480 | tf_op jit(solution)/shard_map/ppermute | solution.py:668
  384.2 10.4 %collective-permute-start.100 = (bf16[384,1536]{1,0:T(8,128)(2,1)S(1)}, bf16[384,1536]{1,0:T(8,128)(2,1)S(1)}, u32[]{:S(2)}, u32[]{:S(2)}) collective-permute-start(bf16[384,1536]{1,0:T(8,128)(2,1)S(1)} %slice.312), channel_id=1, source_target_pairs={{16,20},{20,16},{24,28},{28,24},{17,21},{21,17},{25,29},{29,25},{1... | collective-permute-start | bytes 3538952 | tf_op jit(solution)/shard_map/ppermute | solution.py:668
  387.4 43.8 %collective-permute-start.97 = (bf16[384,1536]{1,0:T(8,128)(2,1)S(1)}, bf16[384,1536]{1,0:T(8,128)(2,1)S(1)}, u32[]{:S(2)}, u32[]{:S(2)}) collective-permute-start(bf16[384,1536]{1,0:T(8,128)(2,1)S(1)} %slice.308), channel_id=1, source_target_pairs={{0,4},{4,0},{8,12},{12,8},{1,5},{5,1},{9,13},{13,9},{2,6},{6,2},{1... | collective-permute-start | bytes 3538952 | tf_op jit(solution)/shard_map/ppermute | solution.py:668
  389.8 37.4 %collective-permute-start.91 = (bf16[384,768]{1,0:T(8,128)(2,1)S(1)}, bf16[384,768]{1,0:T(8,128)(2,1)S(1)}, u32[]{:S(2)}, u32[]{:S(2)}) collective-permute-start(bf16[384,768]{1,0:T(8,128)(2,1)S(1)} %slice.296), channel_id=1, source_target_pairs={{0,4},{4,0},{8,12},{12,8},{1,5},{5,1},{9,13},{13,9},{2,6},{6,2},{1... | collective-permute-start | bytes 1769480 | tf_op jit(solution)/shard_map/ppermute | solution.py:668
  393.9 41.4 %collective-permute-start.95 = (bf16[192,768]{1,0:T(8,128)(2,1)S(1)}, bf16[192,768]{1,0:T(8,128)(2,1)S(1)}, u32[]{:S(2)}, u32[]{:S(2)}) collective-permute-start(bf16[192,768]{1,0:T(8,128)(2,1)S(1)} %slice.302), channel_id=1, source_target_pairs={{16,24},{20,28},{24,16},{28,20},{17,25},{21,29},{25,17},{29,21},{1... | collective-permute-start | bytes 884744 | tf_op jit(solution)/shard_map/ppermute | solution.py:668
  395.8 55.0 %collective-permute-start.101 = (bf16[192,1536]{1,0:T(8,128)(2,1)}, bf16[192,1536]{1,0:T(8,128)(2,1)}, u32[]{:S(2)}, u32[]{:S(2)}) collective-permute-start(bf16[192,1536]{1,0:T(8,128)(2,1)} %slice.314), channel_id=1, source_target_pairs={{16,24},{20,28},{24,16},{28,20},{17,25},{21,29},{25,17},{29,21},{1... | collective-permute-start | bytes 1769480 | tf_op jit(solution)/shard_map/ppermute | solution.py:668
  427.4 21.3 %collective-permute-start.92 = (bf16[192,768]{1,0:T(8,128)(2,1)S(1)}, bf16[192,768]{1,0:T(8,128)(2,1)S(1)}, u32[]{:S(2)}, u32[]{:S(2)}) collective-permute-start(bf16[192,768]{1,0:T(8,128)(2,1)S(1)} %slice.298), channel_id=1, source_target_pairs={{0,8},{4,12},{8,0},{12,4},{1,9},{5,13},{9,1},{13,5},{2,10},{6,14},... | collective-permute-start | bytes 884744 | tf_op jit(solution)/shard_map/ppermute | solution.py:668
  432.3 22.9 %collective-permute-start.98 = (bf16[192,1536]{1,0:T(8,128)(2,1)}, bf16[192,1536]{1,0:T(8,128)(2,1)}, u32[]{:S(2)}, u32[]{:S(2)}) collective-permute-start(bf16[192,1536]{1,0:T(8,128)(2,1)} %slice.310), channel_id=1, source_target_pairs={{0,8},{4,12},{8,0},{12,4},{1,9},{5,13},{9,1},{13,5},{2,10},{6,14},... | collective-permute-start | bytes 1769480 | tf_op jit(solution)/shard_map/ppermute | solution.py:668
  (158 other events, 927.3 us)
